TPU v7x, 256 devices: a whole 4x4x8 slice. The times are simulated.
256 devices in a mesh: ctx: 32 (over y, z), tp: 8 (over x, core).
Axes of the slice: x: 4, y: 4, z: 8, core: 2. Of those that a mesh axis runs over, the one named last changes fastest.
Arguments:
- context_block_rows: bfloat16 [16384, 8192], P('ctx', 'tp'), may hold values from -16 to 16
- query_hidden_rows: bfloat16 [64, 8192], P(None, 'tp'), may hold values from -16 to 16
- query_token_positions: int32 [64], replicated, may hold values from 16384 to 16573, as said below
- query_bound: int32 [64], replicated, may hold values from 1 to 16384, as said below
- query_matrix: bfloat16 [8192, 8192], P('ctx', 'tp'), may hold values from -0.0625 to 0.0625
- key_matrix: bfloat16 [8192, 1024], P('ctx', 'tp'), may hold values from -0.0625 to 0.0625
- value_matrix: bfloat16 [8192, 1024], P('ctx', 'tp'), may hold values from -0.0625 to 0.0625
Outputs:
- block_out: bfloat16 [16384, 8192], P('ctx', 'tp')
- query_out: bfloat16 [64, 8192], P(None, 'tp')
Inputs may be any that keep to these rules, and one draw needn't show every extreme that they name: query_token_positions rise strictly with the index; the first is 16384 and the last 16573. `query_bound`: some query token sees all 16384 context tokens.
All inputs are finite; a program needn't handle non-finite values.
Results may differ from a plain program's by a relative error of at most 0.0059.
The roundings to bfloat16 on the way count: a program that leaves them out, or rounds other values in their place, can miss the bound.
Values may be sent and summed in bfloat16 or wider, within the bound.
A program may use at most 128 MiB of HBM per device.

v0:
```python
import math

import jax
import jax.numpy as jnp
from jax import lax
from jax.sharding import PartitionSpec as P

HEAD_SIZE = 128


def from_root(value, axis, source):
    kept = jnp.where(lax.axis_index(axis) == source, value, 0).astype(value.dtype)
    return lax.psum(kept, axis)


def rope_table(half):
    values = []
    for index in range(half):
        freq = 500000.0 ** (-2.0 * index / (2.0 * half))
        wavelen = 2.0 * math.pi / freq
        if wavelen > 8192.0:
            values.append(freq / 8.0)
        elif wavelen < 2048.0:
            values.append(freq)
        else:
            smooth = (8192.0 / wavelen - 1.0) / 3.0
            values.append((1.0 - smooth) * freq / 8.0 + smooth * freq)
    return values


def apply_rotary(values, token_positions):
    half = values.shape[-1] // 2
    freqs = jnp.asarray(rope_table(half), jnp.float32)
    angle = token_positions.astype(jnp.float32)[:, None] * freqs[None, :]
    cosine = jnp.cos(angle)[:, None, :]
    sine = jnp.sin(angle)[:, None, :]
    first = values[..., :half]
    second = values[..., half:]
    return jnp.concatenate([first * cosine - second * sine, second * cosine + first * sine], -1)


def attend(query_heads_split, keys, values, valid):
    scale = 1.0 / math.sqrt(query_heads_split.shape[-1])
    scores = (
        jnp.einsum("qkgd,skd->qkgs", query_heads_split, keys, preferred_element_type=jnp.float32)
        * scale
    )
    scores = jnp.where(valid[:, None, None, :], scores, -1e30)
    peak = jnp.max(scores, -1)
    weights = jnp.exp(scores - peak[..., None])
    total = jnp.sum(weights, -1)
    mixed = jnp.einsum(
        "qkgs,skd->qkgd", weights.astype(jnp.bfloat16), values, preferred_element_type=jnp.float32
    )
    return (peak, total, mixed)


def on_device(
    context_block_rows,
    query_hidden_rows,
    query_token_positions,
    query_bound,
    query_matrix,
    key_matrix,
    value_matrix,
):
    ctx_index = lax.axis_index("ctx")
    blk = context_block_rows.shape[0]
    qcount = query_hidden_rows.shape[0]
    heads_q = query_matrix.shape[1] // HEAD_SIZE
    heads_kv = key_matrix.shape[1] // HEAD_SIZE
    head_group = heads_q // heads_kv
    whole_rows, whole_query = (
        lax.all_gather(context_block_rows, "tp", axis=1, tiled=True),
        lax.all_gather(query_hidden_rows, "tp", axis=1, tiled=True),
    )
    stacked = jnp.concatenate([whole_rows, whole_query], 0)
    head_rows = blk + qcount
    proj_query = jnp.dot(
        stacked,
        lax.all_gather(query_matrix, "ctx", axis=0, tiled=True),
        preferred_element_type=jnp.float32,
    )
    proj_key = jnp.dot(
        stacked,
        lax.all_gather(key_matrix, "ctx", axis=0, tiled=True),
        preferred_element_type=jnp.float32,
    )
    proj_value = jnp.dot(
        stacked,
        lax.all_gather(value_matrix, "ctx", axis=0, tiled=True),
        preferred_element_type=jnp.float32,
    )
    local_pos = ctx_index * blk + jnp.arange(blk, dtype=jnp.int32)
    k_block = apply_rotary(proj_key[:blk].reshape(blk, heads_kv, HEAD_SIZE), local_pos).astype(
        jnp.bfloat16
    )
    v_block = proj_value[:blk].reshape(blk, heads_kv, HEAD_SIZE).astype(jnp.bfloat16)
    key_token_rows = apply_rotary(
        proj_key[blk:head_rows].reshape(qcount, heads_kv, HEAD_SIZE), query_token_positions
    ).astype(jnp.bfloat16)
    value_token_rows = (
        proj_value[blk:head_rows].reshape(qcount, heads_kv, HEAD_SIZE).astype(jnp.bfloat16)
    )
    anchor_key, anchor_value = (from_root(k_block, "ctx", 0), from_root(v_block, "ctx", 0))
    q_block = apply_rotary(proj_query[:blk].reshape(blk, heads_q, HEAD_SIZE), local_pos).astype(
        jnp.bfloat16
    )
    query_token_rows = (
        apply_rotary(proj_query[blk:].reshape(qcount, heads_q, HEAD_SIZE), query_token_positions)
        .astype(jnp.bfloat16)
        .reshape(qcount, heads_kv, head_group, HEAD_SIZE)
    )
    keys_cat = jnp.concatenate([anchor_key, k_block], 0)
    values_cat = jnp.concatenate([anchor_value, v_block], 0)
    anchor_live = ctx_index > 0
    rows_step = min(blk, 512)
    rows_here = 0 + jnp.arange(rows_step, dtype=jnp.int32)
    valid = jnp.concatenate(
        [
            jnp.broadcast_to(anchor_live, (rows_step, blk)),
            rows_here[:, None] >= jnp.arange(blk, dtype=jnp.int32)[None, :],
        ],
        1,
    )
    query_heads_split = q_block.reshape(rows_step, heads_kv, head_group, HEAD_SIZE)
    peak, total, mixed = attend(query_heads_split, keys_cat, values_cat, valid)
    outputs = (
        (mixed / total[..., None]).astype(jnp.bfloat16).reshape(rows_step, heads_q * HEAD_SIZE)
    )
    valid_ctx = local_pos[None, :] < query_bound[:, None]
    peak, total, mixed = attend(query_token_rows, k_block, v_block, valid_ctx)
    top = lax.pmax(peak, "ctx")
    scaled = jnp.exp(peak - top)
    total_all, mixed_all = lax.psum((total * scaled, mixed * scaled[..., None]), "ctx")
    own = jnp.arange(qcount, dtype=jnp.int32)
    self_peak, self_total, self_mixed = attend(
        query_token_rows, key_token_rows, value_token_rows, own[:, None] >= own[None, :]
    )
    final = jnp.maximum(top, self_peak)
    w_ctx = jnp.exp(top - final)
    w_self = jnp.exp(self_peak - final)
    query_out = (mixed_all * w_ctx[..., None] + self_mixed * w_self[..., None]) / (
        total_all * w_ctx + self_total * w_self
    )[..., None]
    query_out = query_out.astype(jnp.bfloat16).reshape(qcount, heads_q * HEAD_SIZE)
    return (outputs, query_out)


def solution(mesh):
    placed = (
        P("ctx", "tp"),
        P(None, "tp"),
        P(),
        P(),
        P("ctx", "tp"),
        P("ctx", "tp"),
        P("ctx", "tp"),
    )
    return jax.shard_map(
        on_device,
        mesh=mesh,
        in_specs=placed,
        out_specs=(P("ctx", "tp"), P(None, "tp")),
        check_vma=False,
    )
```

profile of v0, /device:TPU:2, one launch (start us, length us, event | category | flops | bytes accessed | tf_op | source)
XLA Modules:
  0.0 689.7 jit_solution(3943614140132584248)
XLA Ops:
  12.3 1.4 broadcast_compare_fusion
  14.5 2.5 multiply_cosine_fusion
  17.0 47.3 %all-gather.6.cloned.1.call-done = bf16[512,8192]{1,0:T(8,128)(2,1)} async-done(((bf16[512,1024]{1,0:T(8,128)(2,1)}), bf16[512,8192]{1,0:T(8,128)(2,1)}) %all-gather.6.cloned.1.call-update) | async-done | bytes 8388624 | tf_op jit(solution)/shard_map/all_gather | solution.py:74
  64.3 7.6 %constant_dynamic-update-slice_fusion.1 = bf16[576,8192]{1,0:T(8,128)(2,1)} fusion(bf16[512,8192]{1,0:T(8,128)(2,1)} %all-gather.6.cloned.1.call-done), kind=kLoop, calls=%fused_computation.100 | loop fusion | bytes 16777216
  71.9 19.5 %all-gather.8.cloned.1.call-done = bf16[64,8192]{1,0:T(8,128)(2,1)} async-done(((bf16[64,1024]{1,0:T(8,128)(2,1)}), bf16[64,8192]{1,0:T(8,128)(2,1)}) %all-gather.8.cloned.1.call-update) | async-done | bytes 1048592 | tf_op jit(solution)/shard_map/all_gather | solution.py:75
  91.4 2.3 constant_dynamic-update-slice_fusion
  93.7 79.8 %all-gather.12.cloned.1.call-done = bf16[8192,128]{1,0:T(8,128)(2,1)} async-done(((bf16[256,128]{1,0:T(8,128)(2,1)}), bf16[8192,128]{1,0:T(8,128)(2,1)}) %all-gather.12.cloned.1.call-update) | async-done | bytes 2097168 | tf_op jit(solution)/shard_map/all_gather | solution.py:86
  173.5 5.8 fusion.83
  182.2 68.9 %all-gather.10.cloned.1.call-done = bf16[8192,128]{1,0:T(8,128)(2,1)} async-done(((bf16[256,128]{1,0:T(8,128)(2,1)}), bf16[8192,128]{1,0:T(8,128)(2,1)}) %all-gather.10.cloned.1.call-update) | async-done | bytes 2097168 | tf_op jit(solution)/shard_map/all_gather | solution.py:91
  251.1 6.9 convolution_convert_fusion
  258.9 132.5 %all-gather.14.cloned.1.call-done = bf16[8192,1024]{1,0:T(8,128)(2,1)} async-done(((bf16[256,1024]{1,0:T(8,128)(2,1)}), bf16[8192,1024]{1,0:T(8,128)(2,1)}) %all-gather.14.cloned.1.call-update) | async-done | bytes 16777232 | tf_op jit(solution)/shard_map/all_gather | solution.py:81
  391.4 14.9 %fusion.84 = f32[576,1024]{1,0:T(8,128)S(1)} fusion(bf16[576,8192]{1,0:T(8,128)(2,1)} %constant_dynamic-update-slice_fusion, bf16[8192,1024]{1,0:T(8,128)(2,1)} %all-gather.14.cloned.1.call-done), kind=kOutput, calls=%fused_computation.126 | convolution fusion | flops 9663676416 | bytes 28573696 | tf_op jit(solution)/shard_map/dot_general | solution.py:79
  406.8 1.4 fusion.81
  409.1 71.4 %pmax.7 = f32[64,1,8]{0,2,1:T(8,128)S(1)} all-reduce(f32[64,1,8]{0,2,1:T(8,128)S(1)} %bitcast.169), channel_id=1, replica_groups=mesh['ctx'=32,'tp'=8] {'ctx'}, use_global_device_ids=true, to_apply=%region_5.6 | all-reduce | flops 512 | bytes 4096 | tf_op jit(solution)/shard_map/pmax | solution.py:133
  481.1 2.0 fusion.79
  484.8 3.5 subtract_convert_fusion
  488.2 47.8 %all-reduce.7.cloned.1.call-done = (bf16[512,1,128]{2,0,1:T(8,128)(2,1)}, bf16[512,1,128]{2,0,1:T(8,128)(2,1)}) async-done(((bf16[512,1,128]{2,0,1:T(8,128)(2,1)}, bf16[512,1,128]{2,0,1:T(8,128)(2,1)}), (bf16[512,1,128]{2,0,1:T(8,128)(2,1)}, bf16[512,1,128]{2,0,1:T(8,128)(2,1)})) %all-reduce.7.cloned.1.call-update) | async-done | bytes 262160 | tf_op jit(solution)/shard_map/psum | solution.py:13
  536.1 10.7 %fusion.2 = (f32[512,8]{0,1:T(8,128)S(1)}, f32[1024,512,8]{1,0,2:T(8,128)}) fusion(pred[512,1024]{0,1:T(8,128)(4,1)} %concatenate.62, bf16[512,8,64]{2,0,1:T(8,128)(2,1)} %get-tuple-element.9, bf16[512,8,64]{2,0,1:T(8,128)(2,1)S(1)} %get-tuple-element.8, bf16[512,1,64]{2,0,1:T(8,128)(2,1)} %copy-done.1, bf16[512,1,64]{2,0,1:T(8,128)(2,1)S(1)} %get-tuple-element.14, ...), kind=kOutput, calls=%fused_computation.4 | convolution fusion | flops 1089204224 | bytes 18628608 | tf_op jit(solution)/shard_map/qkgd,skd->qkgs/dot_general | solution.py:45
  546.8 9.3 %fusion = f32[512,8]{0,1:T(8,128)S(1)} fusion(f32[1024,512,8]{1,0,2:T(8,128)} %get-tuple-element.32, f32[512,8]{0,1:T(8,128)S(1)} %get-tuple-element.31, pred[512,1024]{0,1:T(8,128)(4,1)S(1)} %copy-done), kind=kLoop, calls=%fused_computation.2 | loop fusion | flops 16773120 | bytes 17334272 | tf_op jit(solution)/shard_map/reduce_sum | solution.py:51
  556.5 9.1 %fusion.7 = bf16[1,128,512,8]{2,1,3,0:T(8,128)(2,1)S(1)} fusion(f32[1024,512,8]{1,0,2:T(8,128)} %get-tuple-element.32, f32[512,8]{0,1:T(8,128)S(1)} %get-tuple-element.31, pred[512,1024]{0,1:T(8,128)(4,1)S(1)} %copy-done, f32[512,8]{0,1:T(8,128)S(1)} %fusion, bf16[512,1,128]{2,0,1:T(8,128)(2,1)S(1)} %copy-done.4, bf16[512,1,128]{2,0,1:T(8,128)(2,1)S(1)} %copy-done.10), kind=kOutput, calls=%fused_computation.10 | convolution fusion | flops 1092091904 | bytes 18644992 | tf_op jit(solution)/shard_map/qkgs,skd->qkgd/dot_general | solution.py:52
  565.7 1.3 copy.29
  567.0 72.5 %psum.31 = f32[64,1,8]{0,2,1:T(8,128)S(1)} all-reduce(f32[64,1,8]{0,2,1:T(8,128)S(1)} %copy-done.8), channel_id=1, replica_groups=mesh['ctx'=32,'tp'=8] {'ctx'}, use_global_device_ids=true, to_apply=%region_9.10 | all-reduce | flops 512 | bytes 4096 | tf_op jit(solution)/shard_map/psum | solution.py:135
  639.5 41.2 %all-reduce.5.cloned.1.call-done = f32[64,1,8,128]{3,0,2,1:T(8,128)} async-done(((f32[64,1,8,128]{3,0,2,1:T(8,128)}), f32[64,1,8,128]{3,0,2,1:T(8,128)}) %all-reduce.5.cloned.1.call-update) | async-done | bytes 262160 | tf_op jit(solution)/shard_map/psum | solution.py:135
  680.7 1.3 fusion.19
  (63 shorter events, 14.3 us)
Async XLA Ops:
  7.2 57.1 %all-gather.6.cloned.1.call-start = ((), (), s32[]{:S(2)}) async-start(), calls=%async_computation | async-start | bytes 9437184 | tf_op jit(solution)/shard_map/all_gather | solution.py:74
  7.9 83.5 %all-gather.8.cloned.1.call-start = ((), (), s32[]{:S(2)}) async-start(), calls=%async_computation.1 | async-start | bytes 1179648 | tf_op jit(solution)/shard_map/all_gather | solution.py:75
  8.6 164.9 %all-gather.12.cloned.1.call-start = ((), (), s32[]{:S(2)}) async-start(), calls=%async_computation.3 | async-start | bytes 2162688 | tf_op jit(solution)/shard_map/all_gather | solution.py:86
  9.4 241.7 %all-gather.10.cloned.1.call-start = ((), (), s32[]{:S(2)}) async-start(), calls=%async_computation.2 | async-start | bytes 2162688 | tf_op jit(solution)/shard_map/all_gather | solution.py:91
  10.0 381.4 %all-gather.14.cloned.1.call-start = ((), (), s32[]{:S(2)}) async-start(), calls=%async_computation.4 | async-start | bytes 17301504 | tf_op jit(solution)/shard_map/all_gather | solution.py:81
  10.5 525.5 %all-reduce.7.cloned.1.call-start = ((), (), s32[]{:S(2)}) async-start(), calls=%async_computation.6 | async-start | bytes 524288 | tf_op jit(solution)/shard_map/psum | solution.py:13
  71.9 107.5 %copy-start.9 = (f32[64]{0:T(128)S(1)}, f32[64]{0:T(128)}, u32[]{:S(2)}) copy-start(f32[64]{0:T(128)} %constant.24.clone) | copy-start | bytes 772
  180.6 225.7 %copy-start.1 = (bf16[512,1,64]{2,0,1:T(8,128)(2,1)}, bf16[512,1,64]{2,0,1:T(8,128)(2,1)S(1)}, u32[]{:S(2)}) copy-start(bf16[512,1,64]{2,0,1:T(8,128)(2,1)S(1)} %get-tuple-element.15) | copy-start | bytes 196612
  258.0 133.4 %copy-start.2 = (bf16[576,128]{1,0:T(8,128)(2,1)}, bf16[576,128]{1,0:T(8,128)(2,1)S(1)}, u32[]{:S(2)}) copy-start(bf16[576,128]{1,0:T(8,128)(2,1)S(1)} %convolution_convert_fusion) | copy-start | bytes 442372
  258.8 421.9 %all-reduce.5.cloned.1.call-start = ((), (), s32[]{:S(2)}) async-start(), calls=%async_computation.5 | async-start | bytes 524288 | tf_op jit(solution)/shard_map/psum | solution.py:135
  480.6 2.5 copy-start.7
  480.6 3.1 copy-start.3
  536.1 10.7 %copy-start = (pred[512,1024]{0,1:T(8,128)(4,1)S(1)}, pred[512,1024]{0,1:T(8,128)(4,1)}, u32[]{:S(2)}) copy-start(pred[512,1024]{0,1:T(8,128)(4,1)} %concatenate.62) | copy-start | bytes 1572868
  546.8 9.3 %copy-start.5 = (bf16[64,64]{1,0:T(8,128)(2,1)S(1)}, bf16[64,64]{1,0:T(8,128)(2,1)}, u32[]{:S(2)}) copy-start(bf16[64,64]{1,0:T(8,128)(2,1)} %get-tuple-element.20) | copy-start | bytes 24580
  546.8 9.3 %copy-start.6 = (bf16[64,64]{1,0:T(8,128)(2,1)S(1)}, bf16[64,64]{1,0:T(8,128)(2,1)}, u32[]{:S(2)}) copy-start(bf16[64,64]{1,0:T(8,128)(2,1)} %get-tuple-element.21) | copy-start | bytes 24580
  546.8 9.6 %copy-start.4 = (bf16[512,1,128]{2,0,1:T(8,128)(2,1)S(1)}, bf16[512,1,128]{2,0,1:T(8,128)(2,1)}, u32[]{:S(2)}) copy-start(bf16[512,1,128]{2,0,1:T(8,128)(2,1)} %get-tuple-element.18) | copy-start | bytes 393220
  546.8 9.6 %copy-start.10 = (bf16[512,1,128]{2,0,1:T(8,128)(2,1)S(1)}, bf16[512,1,128]{2,0,1:T(8,128)(2,1)}, u32[]{:S(2)}) copy-start(bf16[512,1,128]{2,0,1:T(8,128)(2,1)} %get-tuple-element.7) | copy-start | bytes 393220
  556.5 10.5 %copy-start.8 = (f32[64,1,8]{0,2,1:T(8,128)S(1)}, f32[64,1,8]{0,2,1:T(8,128)}, u32[]{:S(2)}) copy-start(f32[64,1,8]{0,2,1:T(8,128)} %get-tuple-element.25) | copy-start | bytes 6148
Sparse Core Ops, SparseCore 0:
  9.8 54.4 all-gather.5
  66.1 25.2 all-gather.7
  94.0 79.4 all-gather.11
  176.0 75.1 all-gather.9
  253.6 137.7 all-gather.13
  394.7 141.2 all-reduce.6
  539.5 141.1 all-reduce.4
where the time goes:
time: 690 us
  waiting for transfers between devices  440 us (64%)
  blocking collectives  144 us (21%)
  matrix products  51.5 us (7%)
  other arithmetic  23.5 us (3%)
  local copies, waits for them, and re-layouts  15.8 us (2%)
  between operations  14.4 us (2%)
    all_gather x1, waiting for transfers between devices, on_device(): lax.all_gather(query_matrix, 'ctx', axis=0, tiled=True)  133 us
    all_gather x1, waiting for transfers between devices, on_device(): lax.all_gather(key_matrix, 'ctx', axis=0, tiled=True)  79.8 us
    psum x1, blocking collectives, on_device(): lax.psum((total * scaled, mixed * scaled[..., None]), 'ctx')  72.5 us
    pmax x1, blocking collectives, on_device(): top = lax.pmax(peak, 'ctx')  71.4 us
    all_gather x1, waiting for transfers between devices, on_device(): lax.all_gather(value_matrix, 'ctx', axis=0, tiled=True)  68.9 us
    psum x1, waiting for transfers between devices, from_root(): return lax.psum(kept, axis)  47.8 us
    all_gather x1, waiting for transfers between devices, on_device(): lax.all_gather(context_block_rows, 'tp', axis=1, tiled=True)  47.3 us
    psum x1, waiting for transfers between devices, on_device(): lax.psum((total * scaled, mixed * scaled[..., None]), 'ctx')  41.2 us
  transfers between devices with their start and end apart: 7, of which 7 were waited for; matrix products, arithmetic and copies ran while one was open for 13% of the time, Pallas kernels for 0%

commit v1 on v0

v1 whole, which is shorter than its diff:
```python
import math

import jax
import jax.numpy as jnp
import numpy as np
from jax import lax
from jax.experimental import pallas as pl
from jax.experimental.pallas import tpu as pltpu
from jax.sharding import PartitionSpec as P

MESH = pl.DeviceIdType.MESH
HEAD = 128
NX, NY, NZ = 4, 4, 8
N_CTX = NY * NZ
BLK = 512
QT = 64
ROWS = BLK + QT
SHARD = 256
CUT = 96
REST = SHARD - CUT
BLOCKS = 5
COLS = 256
CHUNK = ROWS // 4
FEATS = 1024
NEG = -1e30
POWER = math.log2(math.e) / math.sqrt(HEAD)
OWN = BLK // N_CTX
F32, BF16 = jnp.float32, jnp.bfloat16


def rope_table(half):
    values = []
    for index in range(half):
        freq = 500000.0 ** (-2.0 * index / (2.0 * half))
        wavelen = 2.0 * math.pi / freq
        if wavelen > 8192.0:
            values.append(freq / 8.0)
        elif wavelen < 2048.0:
            values.append(freq)
        else:
            smooth = (8192.0 / wavelen - 1.0) / 3.0
            values.append((1.0 - smooth) * freq / 8.0 + smooth * freq)
    return values


def bz_at(way, dist):
    return way * 4 + dist - 1


def by_at(off, way, stage):
    return 8 + (off % NZ) * 4 + way * 2 + stage - 1


def ay_at(way, stage):
    return 40 + way * 2 + stage - 1


def az_at(off, way, dist):
    return 44 + (off % NY) * 8 + way * 4 + dist - 1


PLACES = 76
SIGN = (1, -1)


def column(row):
    n = row.shape[1]
    same = lax.broadcasted_iota(jnp.int32, (n, n), 0) == lax.broadcasted_iota(jnp.int32, (n, n), 1)
    return jnp.sum(jnp.where(same, jnp.broadcast_to(row, (n, n)), 0.0), axis=1, keepdims=True)


def dot_nt(a, b):
    return lax.dot_general(a, b, (((1,), (1,)), ((), ())), preferred_element_type=F32)


def kernel(
    x_ref, xq_ref, wq_ref, wk_ref, wv_ref, pos_ref, bound_ref, freq_ref,
    out_ref, qout_ref,
    w_all, x_all, cos_s, sin_s, acc, kv, akv, q_s, qq_s, part, parts,
    local_sem, w_send, w_recv, x_send, x_recv, sib_send, sib_recv, a_send, a_recv,
    p_send, p_recv, r_send, r_recv,
):
    c = lax.axis_index("ctx")
    t = lax.axis_index("tp")
    y, z = lax.div(c, NZ), lax.rem(c, NZ)
    x, core = lax.div(t, 2), lax.rem(t, 2)

    def ctx_at(dy, dz):
        return lax.rem(y + dy + NY, NY) * NZ + lax.rem(z + dz + NZ, NZ)

    def tp_at(dx):
        return lax.rem(x + dx + NX, NX) * 2 + core

    sibling = x * 2 + 1 - core

    locals_ = [
        pltpu.make_async_copy(x_ref, x_all.at[t, pl.ds(0, BLK)], local_sem.at[0]),
        pltpu.make_async_copy(xq_ref, x_all.at[t, pl.ds(BLK, QT)], local_sem.at[1]),
    ]
    own = pl.ds(pl.multiple_of(c * SHARD, SHARD), SHARD)
    locals_.append(pltpu.make_async_copy(wk_ref, w_all.at[0, own, pl.ds(0, HEAD)], local_sem.at[2]))
    locals_.append(pltpu.make_async_copy(wv_ref, w_all.at[0, own, pl.ds(HEAD, HEAD)], local_sem.at[3]))
    for b in range(1, BLOCKS):
        locals_.append(
            pltpu.make_async_copy(
                wq_ref.at[:, pl.ds((b - 1) * COLS, COLS)], w_all.at[b, own], local_sem.at[3 + b]
            )
        )
    for copy in locals_:
        copy.start()

    barrier = pltpu.get_barrier_semaphore()

    @pl.loop(1, N_CTX)
    def _(d):
        pl.semaphore_signal(barrier, inc=1, device_id=(lax.rem(c + d, N_CTX), t), device_id_type=MESH)

    for other in (tp_at(1), tp_at(-1), sibling):
        pl.semaphore_signal(barrier, inc=1, device_id=(c, other), device_id_type=MESH)
    pl.semaphore_wait(barrier, N_CTX - 1 + 3)
    for copy in locals_:
        copy.wait()

    def rows_of(origin, first, count, dist, full, way):
        if dist == full:
            half = count // 2
            first, count = first + (half if way else 0), half
        return pl.ds(pl.multiple_of(origin * SHARD + first, 16), count)

    def w_copy(b, rows, target, line, place):
        piece = w_all.at[b, rows]
        return pltpu.make_async_remote_copy(
            src_ref=piece, dst_ref=piece, send_sem=w_send.at[b, line], recv_sem=w_recv.at[b, place],
            device_id=(target, t), device_id_type=MESH,
        )

    def bz(b, way, dist, hop):
        s = SIGN[way]
        rows = rows_of(ctx_at(0, -s * (dist - 1 + hop)), CUT, REST, dist, 4, way)
        return w_copy(b, rows, ctx_at(0, s), 2 + way, bz_at(way, dist))

    def by(b, off, way, stage, hop):
        s = SIGN[way]
        rows = rows_of(ctx_at(-s * (stage - 1 + hop), off), CUT, REST, stage, 2, way)
        return w_copy(b, rows, ctx_at(s, 0), way, by_at(off, way, stage))

    def ay(b, way, stage, hop):
        s = SIGN[way]
        rows = rows_of(ctx_at(-s * (stage - 1 + hop), 0), 0, CUT, stage, 2, way)
        return w_copy(b, rows, ctx_at(s, 0), way, ay_at(way, stage))

    def az(b, off, way, dist, hop):
        s = SIGN[way]
        rows = rows_of(ctx_at(off, -s * (dist - 1 + hop)), 0, CUT, dist, 4, way)
        return w_copy(b, rows, ctx_at(0, s), 2 + way, az_at(off, way, dist))

    def go(make, *args):
        make(*args, 0).start()

    def got(make, *args):
        make(*args, 1).wait_recv()

    def step(b, s):
        if s == 0:
            for way in (0, 1):
                go(bz, b, way, 1)
                go(ay, b, way, 1)
            for way in (0, 1):
                go(az, b, 0, way, 1)
                go(by, b, 0, way, 1)
            return
        if s <= 4:
            for way in (0, 1):
                got(bz, b, way, s)
                if s < 4:
                    go(bz, b, way, s + 1)
                    go(by, b, -SIGN[way] * s, 0, 1)
                    go(by, b, -SIGN[way] * s, 1, 1)
            if s == 4:
                go(by, b, 4, 0, 1)
                go(by, b, 4, 1, 1)
        if s == 1:
            for way in (0, 1):
                got(ay, b, way, 1)
                go(ay, b, way, 2)
                go(az, b, -SIGN[way], 0, 1)
                go(az, b, -SIGN[way], 1, 1)
        if s == 2:
            got(ay, b, 0, 2)
            got(ay, b, 1, 2)
            go(az, b, 2, 0, 1)
            go(az, b, 2, 1, 1)
        for off, since in ((0, 0), (1, 1), (-1, 1), (2, 2)):
            dist = s - since
            if 1 <= dist <= 4:
                for way in (0, 1):
                    got(az, b, off, way, dist)
                    if dist < 4:
                        go(az, b, off, way, dist + 1)
        for group in range(5):
            offs = (0,) if group == 0 else (4,) if group == 4 else (-group, group)
            stage = s - group
            if 1 <= stage <= 2:
                for off in offs:
                    for way in (0, 1):
                        got(by, b, off, way, stage)
                        if stage == 1:
                            go(by, b, off, way, 2)

    def x_copy(dx, rows, target, send, recv):
        piece = x_all.at[tp_at(dx), rows]
        return pltpu.make_async_remote_copy(
            src_ref=piece, dst_ref=piece, send_sem=send, recv_sem=recv,
            device_id=(c, target), device_id_type=MESH,
        )

    def x_near(way, chunk, hop):
        return x_copy(-SIGN[way] * hop, pl.ds(chunk * CHUNK, CHUNK), tp_at(SIGN[way]), x_send.at[way, chunk], x_recv.at[way, chunk])

    def x_far(way, chunk, hop):
        return x_copy(-SIGN[way] * (1 + hop), pl.ds(chunk * CHUNK, CHUNK), tp_at(SIGN[way]), x_send.at[2, chunk], x_recv.at[2, chunk])

    FAR = ((0, 1), (2, 3))

    def x_across(dx):
        piece = x_all.at[tp_at(dx)]
        return pltpu.make_async_remote_copy(
            src_ref=piece, dst_ref=piece, send_sem=sib_send.at[dx % 4], recv_sem=sib_recv.at[dx % 4],
            device_id=(c, sibling), device_id_type=MESH,
        )

    def x_arrives(dx):
        piece = x_all.at[lax.rem(x + dx + NX, NX) * 2 + 1 - core]
        return pltpu.make_async_remote_copy(
            src_ref=piece, dst_ref=piece, send_sem=sib_send.at[dx % 4], recv_sem=sib_recv.at[dx % 4],
            device_id=(c, sibling), device_id_type=MESH,
        )

    def x_first():
        for way in (0, 1):
            for chunk in FAR[way] + FAR[1 - way]:
                x_near(way, chunk, 0).start()
        x_across(0).start()

    def x_second():
        for way in (0, 1):
            for chunk in FAR[way]:
                x_near(way, chunk, 1).wait_recv()
                x_far(way, chunk, 0).start()

    def x_third():
        for way in (0, 1):
            for chunk in FAR[1 - way]:
                x_near(way, chunk, 1).wait_recv()
            x_across(-SIGN[way]).start()

    def x_fourth():
        for way in (0, 1):
            for chunk in FAR[way]:
                x_far(way, chunk, 1).wait_recv()
        x_across(2).start()

    def x_last():
        for dx in (0, 1, -1, 2):
            x_arrives(dx).wait_recv()

    def angles(first, positions):
        angle = positions * freq_ref[...]
        lane = lax.broadcasted_iota(jnp.int32, angle.shape, 1)
        cosine, sine = jnp.cos(angle), jnp.sin(angle)
        rows = pl.ds(first, angle.shape[0])
        cos_s[rows, :] = cosine
        sin_s[rows, :] = jnp.where(lane < HEAD // 2, -sine, sine)

    def block_angles(first, count):
        place = lax.broadcasted_iota(jnp.int32, (count, HEAD), 0) + (c * BLK + first)
        angles(first, place.astype(F32))

    def query_angles():
        place = column(pos_ref[...].astype(F32))
        angles(BLK, jnp.broadcast_to(place, (QT, HEAD)))

    def rotate(u):
        return u * cos_s[...] + pltpu.roll(u, HEAD // 2, 1) * sin_s[...]

    def project(b):
        acc[...] = jnp.zeros_like(acc)

        @pl.loop(0, 8)
        def _(s):
            acc[...] += jnp.dot(
                x_all[s],
                w_all[b, pl.ds(pl.multiple_of(s * FEATS, FEATS), FEATS), :],
                preferred_element_type=F32,
            )

    def project_kv():
        project(0)
        kv[:, :HEAD] = rotate(acc[:, :HEAD]).astype(BF16)
        kv[:, HEAD:] = acc[:, HEAD:].astype(BF16)

    def project_q(pair):
        project(pair + 1)
        for hh in range(2):
            turned = rotate(acc[:, hh * HEAD : (hh + 1) * HEAD]).astype(BF16)
            q_s[:, hh * HEAD : (hh + 1) * HEAD] = turned[:BLK]
            qq_s[pl.ds(pl.multiple_of((pair * 2 + hh) * QT, QT), QT), :] = turned[BLK:]

    def send_part(owner):
        return pltpu.make_async_remote_copy(
            src_ref=part.at[pl.ds(pl.multiple_of(owner * OWN, OWN), OWN)],
            dst_ref=parts.at[c], send_sem=p_send.at[owner], recv_sem=p_recv.at[c],
            device_id=(owner, t), device_id_type=MESH,
        )

    def query_part(pair):
        rows = pl.ds(pl.multiple_of(pair * 2 * QT, 2 * QT), 2 * QT)
        scores = dot_nt(qq_s[rows, :], kv[:BLK, :HEAD])
        bound = column(bound_ref[...].astype(F32))
        bound = jnp.concatenate([bound, bound], 0)
        place = (lax.broadcasted_iota(jnp.int32, scores.shape, 1) + c * BLK).astype(F32)
        scores = jnp.where(place < bound, scores, NEG)
        peak = jnp.max(scores, 1, keepdims=True)
        weights = jnp.exp2((scores - peak) * POWER)
        total = jnp.sum(weights, 1, keepdims=True)
        mixed = jnp.dot(weights.astype(BF16), kv[:BLK, HEAD:], preferred_element_type=F32)
        lane = lax.broadcasted_iota(jnp.int32, mixed.shape, 1)
        part[rows, :HEAD] = mixed
        part[rows, HEAD:] = jnp.where(lane < HEAD // 2, peak, total)

        @pl.loop(0, 8)
        def _(n):
            owner = pair * 8 + n

            @pl.when(owner != c)
            def _():
                send_part(owner).start()

            @pl.when(owner == c)
            def _():
                parts[c] = part[pl.ds(pl.multiple_of(c * OWN, OWN), OWN), :]

    def attend(pair, hh):
        head = pair * 2 + hh
        bias = jnp.where(c > 0, 0.0, NEG).astype(F32)
        tile = BLK // 2
        for n in range(2):
            span = (n + 1) * tile
            q = q_s[n * tile : span, hh * HEAD : (hh + 1) * HEAD]
            far = dot_nt(q, akv[:, :HEAD])
            near = dot_nt(q, kv[:span, :HEAD])
            row = lax.broadcasted_iota(jnp.int32, near.shape, 0) + n * tile
            near = jnp.where(row >= lax.broadcasted_iota(jnp.int32, near.shape, 1), near, NEG)
            peak = jnp.maximum(
                jnp.max(far, 1, keepdims=True) + bias, jnp.max(near, 1, keepdims=True)
            )
            far = jnp.exp2((far - (peak - bias)) * POWER)
            near = jnp.exp2((near - peak) * POWER)
            total = jnp.sum(far, 1, keepdims=True) + jnp.sum(near, 1, keepdims=True)
            mixed = jnp.dot(far.astype(BF16), akv[:, HEAD:], preferred_element_type=F32)
            mixed += jnp.dot(near.astype(BF16), kv[:span, HEAD:], preferred_element_type=F32)
            out_ref[n * tile : span, pl.ds(pl.multiple_of(head * HEAD, HEAD), HEAD)] = (
                mixed / total
            ).astype(BF16)

    depth = jnp.where(y == 3, 1, y) + jnp.minimum(z, NZ - z)

    def anchor_copy(first, count, target, line, place):
        piece = akv.at[pl.ds(first, count)]
        return pltpu.make_async_remote_copy(
            src_ref=piece, dst_ref=piece, send_sem=a_send.at[line], recv_sem=a_recv.at[place],
            device_id=(target, t), device_id_type=MESH,
        )

    HALF = BLK // 2

    def anchor_sends(act):
        @pl.when((z == 0) & (y < 2))
        def _():
            act(anchor_copy(0, BLK, ctx_at(1, 0), 0, 0))

        @pl.when(c == 0)
        def _():
            act(anchor_copy(0, BLK, ctx_at(-1, 0), 1, 0))

        @pl.when(z < 3)
        def _():
            act(anchor_copy(0, BLK, ctx_at(0, 1), 2, 0))

        @pl.when(z == 3)
        def _():
            act(anchor_copy(0, HALF, ctx_at(0, 1), 2, 0))

        @pl.when((z > 5) | (z == 0))
        def _():
            act(anchor_copy(0, BLK, ctx_at(0, -1), 3, 0))

        @pl.when(z == 5)
        def _():
            act(anchor_copy(HALF, HALF, ctx_at(0, -1), 3, 1))

    def anchor_pass():
        @pl.when(z != 4)
        def _():
            anchor_copy(0, BLK, ctx_at(0, 1), 2, 0).wait_recv()

        @pl.when(z == 4)
        def _():
            anchor_copy(0, HALF, ctx_at(0, 1), 2, 0).wait_recv()
            anchor_copy(HALF, HALF, ctx_at(0, 1), 2, 1).wait_recv()

        anchor_sends(lambda copy: copy.start())

    x_first()

    @pl.loop(0, BLOCKS + 1)
    def _(j):
        for r in range(4):
            if r < 3:

                @pl.when(j >= 1)
                def _():
                    step(j - 1, r + 4)

            @pl.when(j < BLOCKS)
            def _():
                step(j, r)

            @pl.when((depth > 0) & (depth == 4 * j + r - 8))
            def _():
                anchor_pass()

            @pl.when(j == 0)
            def _():
                block_angles(r * (BLK // 4), BLK // 4)
                if r == 3:
                    query_angles()
                    x_second()

            @pl.when(j == 1)
            def _():
                if r == 1:
                    x_third()
                if r == 3:
                    x_fourth()

            if r == 0:

                @pl.when(j == 2)
                def _():
                    x_last()
                    project_kv()

                    @pl.when(c == 0)
                    def _():
                        akv[...] = kv[:BLK, :]
                        anchor_sends(lambda copy: copy.start())

            if r == 2:

                @pl.when(j == 3)
                def _():
                    attend(0, 0)
                    attend(0, 1)

            if r == 0:

                @pl.when(j >= 4)
                def _():
                    attend(j - 3, 0)
                    attend(j - 3, 1)

            if r == 3:

                @pl.when(j >= 2)
                def _():
                    project_q(j - 2)
                    query_part(j - 2)

    attend(3, 0)
    attend(3, 1)

    @pl.loop(0, N_CTX)
    def _(n):
        @pl.when(n != c)
        def _():
            piece = parts.at[n]
            pltpu.make_async_remote_copy(
                src_ref=piece, dst_ref=piece, send_sem=p_send.at[n], recv_sem=p_recv.at[n],
                device_id=(n, t), device_id_type=MESH,
            ).wait_recv()

    peaks = parts[:, :, HEAD : HEAD + 1]
    top = jnp.max(peaks, 0)
    scaled = jnp.exp2((peaks - top[None]) * POWER)
    total_all = jnp.sum(parts[:, :, HEAD + HEAD // 2 : HEAD + HEAD // 2 + 1] * scaled, 0)
    mixed_all = jnp.sum(parts[:, :, :HEAD] * scaled, 0)

    first = lax.rem(c, QT // OWN) * OWN
    mine = qq_s[pl.ds(pl.multiple_of(c * OWN, OWN), OWN), :]
    scores = dot_nt(mine, kv[BLK:, :HEAD])
    row = lax.broadcasted_iota(jnp.int32, scores.shape, 0) + first
    scores = jnp.where(row >= lax.broadcasted_iota(jnp.int32, scores.shape, 1), scores, NEG)
    peak = jnp.max(scores, 1, keepdims=True)
    weights = jnp.exp2((scores - peak) * POWER)
    total = jnp.sum(weights, 1, keepdims=True)
    mixed = jnp.dot(weights.astype(BF16), kv[BLK:, HEAD:], preferred_element_type=F32)
    final = jnp.maximum(top, peak)
    w_ctx = jnp.exp2((top - final) * POWER)
    w_self = jnp.exp2((peak - final) * POWER)
    done = (mixed_all * w_ctx + mixed * w_self) / (total_all * w_ctx + total * w_self)

    def result_at(n):
        return qout_ref.at[
            pl.ds(pl.multiple_of(lax.rem(n, QT // OWN) * OWN, OWN), OWN),
            pl.ds(pl.multiple_of(lax.div(n, QT // OWN) * HEAD, HEAD), HEAD),
        ]

    def result_copy(source, target):
        piece = result_at(source)
        return pltpu.make_async_remote_copy(
            src_ref=piece, dst_ref=piece, send_sem=r_send.at[target], recv_sem=r_recv.at[source],
            device_id=(target, t), device_id_type=MESH,
        )

    result_at(c)[...] = done.astype(BF16)

    @pl.loop(1, N_CTX)
    def _(d):
        result_copy(c, lax.rem(c + d, N_CTX)).start()

    @pl.loop(1, N_CTX)
    def _(d):
        other = lax.rem(c + d, N_CTX)
        result_copy(other, other).wait_recv()

    @pl.loop(1, N_CTX)
    def _(d):
        other = lax.rem(c + d, N_CTX)
        result_copy(c, other).wait_send()
        send_part(other).wait_send()

    @pl.loop(0, BLOCKS)
    def _(b):
        for line in range(4):
            rows = (3 * CUT // 2 + 8 * (3 * REST // 2)) if line < 2 else 7 * REST // 2 + 4 * (7 * CUT // 2)
            w_copy(b, pl.ds(0, rows), ctx_at(1, 0), line, 0).wait_send()

    for way in (0, 1):
        for chunk in range(4):
            x_near(way, chunk, 0).wait_send()
        for chunk in FAR[way]:
            x_far(way, chunk, 0).wait_send()
    for dx in (0, 1, -1, 2):
        x_across(dx).wait_send()
    anchor_sends(lambda copy: copy.wait_send())


def on_device(rows, query_rows, positions, bound, wq, wk, wv):
    freq = np.asarray(rope_table(HEAD // 2) * 2, np.float32)[None]
    anywhere = pl.BlockSpec(memory_space=pl.ANY)
    vmem = pl.BlockSpec(memory_space=pltpu.VMEM)
    dma = pltpu.SemaphoreType.DMA
    return pl.pallas_call(
        kernel,
        out_shape=(
            jax.ShapeDtypeStruct((BLK, 8 * HEAD), BF16),
            jax.ShapeDtypeStruct((QT, 8 * HEAD), BF16),
        ),
        in_specs=[anywhere] * 5 + [vmem] * 3,
        out_specs=(vmem, vmem),
        scratch_shapes=[
            pltpu.VMEM((BLOCKS, N_CTX * SHARD, COLS), BF16),
            pltpu.VMEM((8, ROWS, FEATS), BF16),
            pltpu.VMEM((ROWS, HEAD), F32),
            pltpu.VMEM((ROWS, HEAD), F32),
            pltpu.VMEM((ROWS, COLS), F32),
            pltpu.VMEM((ROWS, COLS), BF16),
            pltpu.VMEM((BLK, COLS), BF16),
            pltpu.VMEM((BLK, COLS), BF16),
            pltpu.VMEM((8 * QT, HEAD), BF16),
            pltpu.VMEM((8 * QT, 2 * HEAD), F32),
            pltpu.VMEM((N_CTX, OWN, 2 * HEAD), F32),
            dma((3 + BLOCKS,)),
            dma((BLOCKS, 4)),
            dma((BLOCKS, PLACES)),
            dma((3, 4)),
            dma((3, 4)),
            dma((4,)),
            dma((4,)),
            dma((4,)),
            dma((2,)),
            dma((N_CTX,)),
            dma((N_CTX,)),
            dma((N_CTX,)),
            dma((N_CTX,)),
        ],
        compiler_params=pltpu.CompilerParams(
            collective_id=0, has_side_effects=True, vmem_limit_bytes=56 << 20
        ),
        name="star_prefill",
    )(rows, query_rows, wq, wk, wv, positions[None], bound[None], freq)


def solution(mesh):
    placed = (
        P("ctx", "tp"),
        P(None, "tp"),
        P(),
        P(),
        P("ctx", "tp"),
        P("ctx", "tp"),
        P("ctx", "tp"),
    )
    return jax.shard_map(
        on_device,
        mesh=mesh,
        in_specs=placed,
        out_specs=(P("ctx", "tp"), P(None, "tp")),
        check_vma=False,
    )
```

time: 690 us -> 179 us (0.26)
  waiting for transfers between devices: 440 us -> 0 us
  Pallas kernels: 0 us -> 175 us
  blocking collectives: 144 us -> 0 us
  matrix products: 51.5 us -> 0 us
  other arithmetic: 23.5 us -> 0 us
  between operations: 14.4 us -> 0.65 us
  local copies, waits for them, and re-layouts: 15.8 us -> 2.96 us
    all_gather x5 -> x0, waiting for transfers between devices: 348 us -> none  [the longest x1 133 us: on_device(): lax.all_gather(query_matrix, 'ctx', axis=0, tiled=True)]
    pallas_call x0 -> x1, Pallas kernels: none -> 175 us  [on_device(): pl.pallas_call(kernel, out_shape=(jax.ShapeDtypeStruct((BLK, 8 * HEAD), B...]
    psum x2 -> x0, waiting for transfers between devices: 89 us -> none  [the longest x1 47.8 us: from_root(): return lax.psum(kept, axis)]
    psum x1 -> x0, blocking collectives: 72.5 us -> none  [on_device(): lax.psum((total * scaled, mixed * scaled[..., None]), 'ctx')]
    pmax x1 -> x0, blocking collectives: 71.4 us -> none  [on_device(): top = lax.pmax(peak, 'ctx')]
    dot_general x9 -> x0, matrix products: 51.5 us -> none  [the longest x1 14.9 us: on_device(): jnp.dot(stacked, lax.all_gather(query_matrix, 'ctx', axis=0, tiled=True),...]
    reduce_sum x3 -> x0, other arithmetic: 10.3 us -> none  [attend(): total = jnp.sum(weights, -1)]
    unnamed x29 -> x4, local copies, waits for them, and re-layouts: 10.3 us -> 2.96 us
  transfers between devices with their start and end apart: 7 -> 0, of which waited for: 7 -> 0; matrix products, arithmetic and copies ran while one was open for 13% -> 0% of each run, Pallas kernels for 0% -> 0%
where the time goes in v1:
time: 179 us
  Pallas kernels  175 us (98%)
  local copies, waits for them, and re-layouts  2.96 us (2%)
    pallas_call x1, Pallas kernels, on_device(): pl.pallas_call(kernel, out_shape=(jax.ShapeDtypeStruct((BLK, 8 * HEAD), B...  175 us

profile of v1, /device:TPU:2, one launch (start us, length us, event | category | flops | bytes accessed | tf_op | source)
XLA Modules:
  0.0 178.6 jit_solution(11212064277726953040)
XLA Ops:
  0.6 175.0 %star_prefill.1 = (bf16[512,1024]{1,0:T(8,128)(2,1)}, bf16[64,1024]{1,0:T(8,128)(2,1)}) custom-call(bf16[512,1024]{1,0:T(8,128)(2,1)} %x_ref.1, bf16[64,1024]{1,0:T(8,128)(2,1)} %xq_ref.1, bf16[256,1024]{1,0:T(8,128)(2,1)} %wq_ref.1, bf16[256,128]{1,0:T(8,128)(2,1)} %wk_ref.1, bf16[256,128]{1,0:T(8,128)(2,1)} %wv_ref.1, s32[1,64]{1,0:T(1,128)} %bitcast.2, ...), custom_call_target="tpu_custom_call" | custom-call | tf_op jit(solution)/shard_map/star_prefill/pallas_call | solution.py:564
  175.6 0.0 copy-start
  175.6 2.3 %copy.12 = bf16[512,1024]{1,0:T(8,128)(2,1)} copy(bf16[512,1024]{1,0:T(8,128)(2,1)} %get-tuple-element.4) | data formatting | bytes 2097152
  177.9 0.0 copy-done
  177.9 0.7 copy.13
Async XLA Ops:
  175.6 2.3 %copy-start = (bf16[64,1024]{1,0:T(8,128)(2,1)S(1)}, bf16[64,1024]{1,0:T(8,128)(2,1)}, u32[]{:S(2)}) copy-start(bf16[64,1024]{1,0:T(8,128)(2,1)} %get-tuple-element.5) | copy-start | bytes 393220

commit v2 on v1

--- a/solution.py
+++ b/solution.py
@@ -18,7 +18,9 @@
 SHARD = 256
 CUT = 96
 REST = SHARD - CUT
-BLOCKS = 5
+BLOCKS = 4
+TAILS = 2
+PAIRS = 3
 COLS = 256
 CHUNK = ROWS // 4
 FEATS = 1024
@@ -43,23 +45,23 @@
     return values
 
 
-def bz_at(way, dist):
-    return way * 4 + dist - 1
-
-
-def by_at(off, way, stage):
-    return 8 + (off % NZ) * 4 + way * 2 + stage - 1
-
-
-def ay_at(way, stage):
-    return 40 + way * 2 + stage - 1
-
-
-def az_at(off, way, dist):
-    return 44 + (off % NY) * 8 + way * 4 + dist - 1
-
-
-PLACES = 76
+def bz_at(dist):
+    return dist - 1
+
+
+def by_at(off, stage):
+    return 4 + (off % NZ) * 2 + stage - 1
+
+
+def ay_at(stage):
+    return 20 + stage - 1
+
+
+def az_at(off, dist):
+    return 22 + (off % NY) * 4 + dist - 1
+
+
+PLACES = 38
 SIGN = (1, -1)
 
 
@@ -76,7 +78,7 @@
 def kernel(
     x_ref, xq_ref, wq_ref, wk_ref, wv_ref, pos_ref, bound_ref, freq_ref,
     out_ref, qout_ref,
-    w_all, x_all, cos_s, sin_s, acc, kv, akv, q_s, qq_s, part, parts,
+    w_all, w_tail, x_all, cos_s, sin_s, acc, kv, akv, q_s, qq_s, part, parts,
     local_sem, w_send, w_recv, x_send, x_recv, sib_send, sib_recv, a_send, a_recv,
     p_send, p_recv, r_send, r_recv,
 ):
@@ -106,6 +108,12 @@
                 wq_ref.at[:, pl.ds((b - 1) * COLS, COLS)], w_all.at[b, own], local_sem.at[3 + b]
             )
         )
+    for b in range(TAILS):
+        locals_.append(
+            pltpu.make_async_copy(
+                wq_ref.at[:, pl.ds(PAIRS * COLS + b * HEAD, HEAD)], w_tail.at[b, own], local_sem.at[3 + BLOCKS + b]
+            )
+        )
     for copy in locals_:
         copy.start()
 
@@ -127,85 +135,85 @@
             first, count = first + (half if way else 0), half
         return pl.ds(pl.multiple_of(origin * SHARD + first, 16), count)
 
-    def w_copy(b, rows, target, line, place):
-        piece = w_all.at[b, rows]
+    def w_copy(blk, rows, target, line, place):
+        ref, sem = blk
+        piece = ref.at[rows]
         return pltpu.make_async_remote_copy(
-            src_ref=piece, dst_ref=piece, send_sem=w_send.at[b, line], recv_sem=w_recv.at[b, place],
+            src_ref=piece, dst_ref=piece, send_sem=w_send.at[sem, line], recv_sem=w_recv.at[sem, place],
             device_id=(target, t), device_id_type=MESH,
         )
 
-    def bz(b, way, dist, hop):
+    def wide(j):
+        return w_all.at[j], j
+
+    def tail(n):
+        return w_tail.at[n], BLOCKS + n
+
+    def bz(blk, way, dist):
         s = SIGN[way]
-        rows = rows_of(ctx_at(0, -s * (dist - 1 + hop)), CUT, REST, dist, 4, way)
-        return w_copy(b, rows, ctx_at(0, s), 2 + way, bz_at(way, dist))
-
-    def by(b, off, way, stage, hop):
+        rows = rows_of(ctx_at(0, -s * (dist - 1)), CUT, REST, dist, 4, way)
+        w_copy(blk, rows, ctx_at(0, s), 2 + way, bz_at(dist)).start()
+
+    def by(blk, off, way, stage):
         s = SIGN[way]
-        rows = rows_of(ctx_at(-s * (stage - 1 + hop), off), CUT, REST, stage, 2, way)
-        return w_copy(b, rows, ctx_at(s, 0), way, by_at(off, way, stage))
-
-    def ay(b, way, stage, hop):
+        rows = rows_of(ctx_at(-s * (stage - 1), off), CUT, REST, stage, 2, way)
+        w_copy(blk, rows, ctx_at(s, 0), way, by_at(off, stage)).start()
+
+    def ay(blk, way, stage):
         s = SIGN[way]
-        rows = rows_of(ctx_at(-s * (stage - 1 + hop), 0), 0, CUT, stage, 2, way)
-        return w_copy(b, rows, ctx_at(s, 0), way, ay_at(way, stage))
-
-    def az(b, off, way, dist, hop):
+        rows = rows_of(ctx_at(-s * (stage - 1), 0), 0, CUT, stage, 2, way)
+        w_copy(blk, rows, ctx_at(s, 0), way, ay_at(stage)).start()
+
+    def az(blk, off, way, dist):
         s = SIGN[way]
-        rows = rows_of(ctx_at(off, -s * (dist - 1 + hop)), 0, CUT, dist, 4, way)
-        return w_copy(b, rows, ctx_at(0, s), 2 + way, az_at(off, way, dist))
-
-    def go(make, *args):
-        make(*args, 0).start()
-
-    def got(make, *args):
-        make(*args, 1).wait_recv()
-
-    def step(b, s):
+        rows = rows_of(ctx_at(off, -s * (dist - 1)), 0, CUT, dist, 4, way)
+        w_copy(blk, rows, ctx_at(0, s), 2 + way, az_at(off, dist)).start()
+
+    def both(make, blk, *args):
+        *front, last = args
+        for way in (0, 1):
+            make(blk, *front, way, last)
+
+    def got(blk, place, count):
+        w_copy(blk, pl.ds(0, count), ctx_at(1, 0), 0, place).wait_recv()
+
+    def step(blk, s):
         if s == 0:
-            for way in (0, 1):
-                go(bz, b, way, 1)
-                go(ay, b, way, 1)
-            for way in (0, 1):
-                go(az, b, 0, way, 1)
-                go(by, b, 0, way, 1)
+            both(bz, blk, 1)
+            both(ay, blk, 1)
+            both(az, blk, 0, 1)
+            both(by, blk, 0, 1)
             return
         if s <= 4:
-            for way in (0, 1):
-                got(bz, b, way, s)
-                if s < 4:
-                    go(bz, b, way, s + 1)
-                    go(by, b, -SIGN[way] * s, 0, 1)
-                    go(by, b, -SIGN[way] * s, 1, 1)
-            if s == 4:
-                go(by, b, 4, 0, 1)
-                go(by, b, 4, 1, 1)
+            got(blk, bz_at(s), 2 * REST if s < 4 else REST)
+            if s < 4:
+                both(bz, blk, s + 1)
+                both(by, blk, -s, 1)
+                both(by, blk, s, 1)
+            else:
+                both(by, blk, 4, 1)
         if s == 1:
-            for way in (0, 1):
-                got(ay, b, way, 1)
-                go(ay, b, way, 2)
-                go(az, b, -SIGN[way], 0, 1)
-                go(az, b, -SIGN[way], 1, 1)
+            got(blk, ay_at(1), 2 * CUT)
+            both(ay, blk, 2)
+            both(az, blk, -1, 1)
+            both(az, blk, 1, 1)
         if s == 2:
-            got(ay, b, 0, 2)
-            got(ay, b, 1, 2)
-            go(az, b, 2, 0, 1)
-            go(az, b, 2, 1, 1)
+            got(blk, ay_at(2), CUT)
+            both(az, blk, 2, 1)
         for off, since in ((0, 0), (1, 1), (-1, 1), (2, 2)):
             dist = s - since
             if 1 <= dist <= 4:
-                for way in (0, 1):
-                    got(az, b, off, way, dist)
-                    if dist < 4:
-                        go(az, b, off, way, dist + 1)
+                got(blk, az_at(off, dist), 2 * CUT if dist < 4 else CUT)
+                if dist < 4:
+                    both(az, blk, off, dist + 1)
         for group in range(5):
             offs = (0,) if group == 0 else (4,) if group == 4 else (-group, group)
             stage = s - group
             if 1 <= stage <= 2:
                 for off in offs:
-                    for way in (0, 1):
-                        got(by, b, off, way, stage)
-                        if stage == 1:
-                            go(by, b, off, way, 2)
+                    got(blk, by_at(off, stage), 2 * REST if stage == 1 else REST)
+                    if stage == 1:
+                        both(by, blk, off, 2)
 
     def x_copy(dx, rows, target, send, recv):
         piece = x_all.at[tp_at(dx), rows]
@@ -280,31 +288,38 @@
         place = column(pos_ref[...].astype(F32))
         angles(BLK, jnp.broadcast_to(place, (QT, HEAD)))
 
-    def rotate(u):
-        return u * cos_s[...] + pltpu.roll(u, HEAD // 2, 1) * sin_s[...]
-
-    def project(b):
-        acc[...] = jnp.zeros_like(acc)
+    def project(weights, first, count, columns):
+        acc[first : first + count, :columns] = jnp.zeros((count, columns), F32)
 
         @pl.loop(0, 8)
         def _(s):
-            acc[...] += jnp.dot(
-                x_all[s],
-                w_all[b, pl.ds(pl.multiple_of(s * FEATS, FEATS), FEATS), :],
+            acc[first : first + count, :columns] += jnp.dot(
+                x_all[s, first : first + count],
+                weights[pl.ds(pl.multiple_of(s * FEATS, FEATS), FEATS), :],
                 preferred_element_type=F32,
             )
 
+    def rotate(first, count, lane):
+        u = acc[first : first + count, lane : lane + HEAD]
+        turned = u * cos_s[first : first + count] + pltpu.roll(u, HEAD // 2, 1) * sin_s[first : first + count]
+        return turned.astype(BF16)
+
     def project_kv():
-        project(0)
-        kv[:, :HEAD] = rotate(acc[:, :HEAD]).astype(BF16)
+        project(w_all.at[0], 0, ROWS, COLS)
+        kv[:, :HEAD] = rotate(0, ROWS, 0)
         kv[:, HEAD:] = acc[:, HEAD:].astype(BF16)
 
-    def project_q(pair):
-        project(pair + 1)
+    def keep_block(head, lane):
+        q_s[head] = rotate(0, BLK, lane)
+
+    def keep_query(head, lane):
+        qq_s[pl.ds(pl.multiple_of(head * QT, QT), QT), :] = rotate(BLK, QT, lane)
+
+    def project_pair(pair):
+        project(w_all.at[pair + 1], 0, ROWS, COLS)
         for hh in range(2):
-            turned = rotate(acc[:, hh * HEAD : (hh + 1) * HEAD]).astype(BF16)
-            q_s[:, hh * HEAD : (hh + 1) * HEAD] = turned[:BLK]
-            qq_s[pl.ds(pl.multiple_of((pair * 2 + hh) * QT, QT), QT), :] = turned[BLK:]
+            keep_block(pair * 2 + hh, hh * HEAD)
+            keep_query(pair * 2 + hh, hh * HEAD)
 
     def send_part(owner):
         return pltpu.make_async_remote_copy(
@@ -313,11 +328,11 @@
             device_id=(owner, t), device_id_type=MESH,
         )
 
-    def query_part(pair):
-        rows = pl.ds(pl.multiple_of(pair * 2 * QT, 2 * QT), 2 * QT)
+    def query_part(head, heads):
+        rows = pl.ds(pl.multiple_of(head * QT, QT), heads * QT)
         scores = dot_nt(qq_s[rows, :], kv[:BLK, :HEAD])
         bound = column(bound_ref[...].astype(F32))
-        bound = jnp.concatenate([bound, bound], 0)
+        bound = jnp.concatenate([bound] * heads, 0)
         place = (lax.broadcasted_iota(jnp.int32, scores.shape, 1) + c * BLK).astype(F32)
         scores = jnp.where(place < bound, scores, NEG)
         peak = jnp.max(scores, 1, keepdims=True)
@@ -328,9 +343,9 @@
         part[rows, :HEAD] = mixed
         part[rows, HEAD:] = jnp.where(lane < HEAD // 2, peak, total)
 
-        @pl.loop(0, 8)
+        @pl.loop(0, heads * QT // OWN)
         def _(n):
-            owner = pair * 8 + n
+            owner = head * (QT // OWN) + n
 
             @pl.when(owner != c)
             def _():
@@ -340,13 +355,12 @@
             def _():
                 parts[c] = part[pl.ds(pl.multiple_of(c * OWN, OWN), OWN), :]
 
-    def attend(pair, hh):
-        head = pair * 2 + hh
+    def attend(head):
         bias = jnp.where(c > 0, 0.0, NEG).astype(F32)
         tile = BLK // 2
         for n in range(2):
             span = (n + 1) * tile
-            q = q_s[n * tile : span, hh * HEAD : (hh + 1) * HEAD]
+            q = q_s[head, n * tile : span, :]
             far = dot_nt(q, akv[:, :HEAD])
             near = dot_nt(q, kv[:span, :HEAD])
             row = lax.broadcasted_iota(jnp.int32, near.shape, 0) + n * tile
@@ -372,63 +386,84 @@
             device_id=(target, t), device_id_type=MESH,
         )
 
+    PIECE = BLK // 4
     HALF = BLK // 2
 
-    def anchor_sends(act):
+    def anchor_lines(act):
         @pl.when((z == 0) & (y < 2))
         def _():
-            act(anchor_copy(0, BLK, ctx_at(1, 0), 0, 0))
+            act(ctx_at(1, 0), 0)
 
         @pl.when(c == 0)
         def _():
-            act(anchor_copy(0, BLK, ctx_at(-1, 0), 1, 0))
+            act(ctx_at(-1, 0), 1)
 
         @pl.when(z < 3)
         def _():
-            act(anchor_copy(0, BLK, ctx_at(0, 1), 2, 0))
+            act(ctx_at(0, 1), 2)
+
+        @pl.when((z > 5) | (z == 0))
+        def _():
+            act(ctx_at(0, -1), 3)
+
+    def anchor_piece(k, target, line):
+        return anchor_copy(pl.multiple_of(k * PIECE, PIECE), PIECE, target, line, k)
+
+    def anchor_step(g):
+        k = g - depth
+
+        @pl.when((k >= 0) & (k < 4))
+        def _():
+            @pl.when(depth > 0)
+            def _():
+                anchor_piece(k, ctx_at(0, 1), 2).wait_recv()
+
+            anchor_lines(lambda target, line: anchor_piece(k, target, line).start())
+
+            @pl.when((z == 3) & (k < 2))
+            def _():
+                anchor_piece(k, ctx_at(0, 1), 2).start()
+
+            @pl.when((z == 5) & (k >= 2))
+            def _():
+                anchor_piece(k, ctx_at(0, -1), 3).start()
+
+    def anchor_end():
+        anchor_lines(lambda target, line: anchor_copy(0, BLK, target, line, 0).wait_send())
 
         @pl.when(z == 3)
         def _():
-            act(anchor_copy(0, HALF, ctx_at(0, 1), 2, 0))
-
-        @pl.when((z > 5) | (z == 0))
-        def _():
-            act(anchor_copy(0, BLK, ctx_at(0, -1), 3, 0))
+            anchor_copy(0, HALF, ctx_at(0, 1), 2, 0).wait_send()
 
         @pl.when(z == 5)
         def _():
-            act(anchor_copy(HALF, HALF, ctx_at(0, -1), 3, 1))
-
-    def anchor_pass():
-        @pl.when(z != 4)
-        def _():
-            anchor_copy(0, BLK, ctx_at(0, 1), 2, 0).wait_recv()
-
-        @pl.when(z == 4)
-        def _():
-            anchor_copy(0, HALF, ctx_at(0, 1), 2, 0).wait_recv()
-            anchor_copy(HALF, HALF, ctx_at(0, 1), 2, 1).wait_recv()
-
-        anchor_sends(lambda copy: copy.start())
+            anchor_copy(0, HALF, ctx_at(0, -1), 3, 0).wait_send()
 
     x_first()
 
-    @pl.loop(0, BLOCKS + 1)
+    @pl.loop(0, BLOCKS)
     def _(j):
         for r in range(4):
             if r < 3:
 
                 @pl.when(j >= 1)
                 def _():
-                    step(j - 1, r + 4)
-
-            @pl.when(j < BLOCKS)
-            def _():
-                step(j, r)
-
-            @pl.when((depth > 0) & (depth == 4 * j + r - 8))
-            def _():
-                anchor_pass()
+                    step(wide(j - 1), r + 4)
+
+            step(wide(j), r)
+
+            if r == 0:
+
+                @pl.when(j == 2)
+                def _():
+                    x_last()
+                    project_kv()
+
+                    @pl.when(c == 0)
+                    def _():
+                        akv[...] = kv[:BLK, :]
+
+            anchor_step(4 * j + r - 8)
 
             @pl.when(j == 0)
             def _():
@@ -444,41 +479,49 @@
                 if r == 3:
                     x_fourth()
 
-            if r == 0:
-
-                @pl.when(j == 2)
-                def _():
-                    x_last()
-                    project_kv()
-
-                    @pl.when(c == 0)
-                    def _():
-                        akv[...] = kv[:BLK, :]
-                        anchor_sends(lambda copy: copy.start())
-
-            if r == 2:
-
-                @pl.when(j == 3)
-                def _():
-                    attend(0, 0)
-                    attend(0, 1)
-
-            if r == 0:
-
-                @pl.when(j >= 4)
-                def _():
-                    attend(j - 3, 0)
-                    attend(j - 3, 1)
-
             if r == 3:
 
                 @pl.when(j >= 2)
                 def _():
-                    project_q(j - 2)
-                    query_part(j - 2)
-
-    attend(3, 0)
-    attend(3, 1)
+                    project_pair(j - 2)
+                    query_part((j - 2) * 2, 2)
+
+    for r in range(4):
+        if r < 3:
+            step(wide(BLOCKS - 1), r + 4)
+        step(tail(0), r)
+        if r < 2:
+            anchor_step(4 * BLOCKS + r - 8)
+        if r == 3:
+            project_pair(2)
+            query_part(4, 2)
+        else:
+
+            @pl.loop(0, 2)
+            def _(hh):
+                if r > 0:
+                    attend((r - 1) * 2 + hh)
+
+    for r in range(4):
+        if r < 3:
+            step(tail(0), r + 4)
+        step(tail(1), r)
+        if r < 2:
+            attend(4 + r)
+        if r == 3:
+            project(w_tail.at[0], 0, ROWS, HEAD)
+            keep_block(6, 0)
+            keep_query(6, 0)
+            query_part(6, 1)
+    for r in range(3):
+        step(tail(1), r + 4)
+        if r == 0:
+            attend(6)
+    project(w_tail.at[1], BLK, QT, HEAD)
+    keep_query(7, 0)
+    query_part(7, 1)
+    project(w_tail.at[1], 0, BLK, HEAD)
+    keep_block(7, 0)
 
     @pl.loop(0, N_CTX)
     def _(n):
@@ -529,6 +572,8 @@
     def _(d):
         result_copy(c, lax.rem(c + d, N_CTX)).start()
 
+    attend(7)
+
     @pl.loop(1, N_CTX)
     def _(d):
         other = lax.rem(c + d, N_CTX)
@@ -540,11 +585,17 @@
         result_copy(c, other).wait_send()
         send_part(other).wait_send()
 
+    def w_end(blk):
+        for line in range(4):
+            rows = (3 * CUT // 2 + 8 * (3 * REST // 2)) if line < 2 else 7 * REST // 2 + 4 * (7 * CUT // 2)
+            w_copy(blk, pl.ds(0, rows), ctx_at(1, 0), line, 0).wait_send()
+
     @pl.loop(0, BLOCKS)
     def _(b):
-        for line in range(4):
-            rows = (3 * CUT // 2 + 8 * (3 * REST // 2)) if line < 2 else 7 * REST // 2 + 4 * (7 * CUT // 2)
-            w_copy(b, pl.ds(0, rows), ctx_at(1, 0), line, 0).wait_send()
+        w_end(wide(b))
+
+    for b in range(TAILS):
+        w_end(tail(b))
 
     for way in (0, 1):
         for chunk in range(4):
@@ -553,7 +604,7 @@
             x_far(way, chunk, 0).wait_send()
     for dx in (0, 1, -1, 2):
         x_across(dx).wait_send()
-    anchor_sends(lambda copy: copy.wait_send())
+    anchor_end()
 
 
 def on_device(rows, query_rows, positions, bound, wq, wk, wv):
@@ -571,25 +622,26 @@
         out_specs=(vmem, vmem),
         scratch_shapes=[
             pltpu.VMEM((BLOCKS, N_CTX * SHARD, COLS), BF16),
+            pltpu.VMEM((TAILS, N_CTX * SHARD, HEAD), BF16),
             pltpu.VMEM((8, ROWS, FEATS), BF16),
             pltpu.VMEM((ROWS, HEAD), F32),
             pltpu.VMEM((ROWS, HEAD), F32),
             pltpu.VMEM((ROWS, COLS), F32),
             pltpu.VMEM((ROWS, COLS), BF16),
             pltpu.VMEM((BLK, COLS), BF16),
-            pltpu.VMEM((BLK, COLS), BF16),
+            pltpu.VMEM((8, BLK, HEAD), BF16),
             pltpu.VMEM((8 * QT, HEAD), BF16),
             pltpu.VMEM((8 * QT, 2 * HEAD), F32),
             pltpu.VMEM((N_CTX, OWN, 2 * HEAD), F32),
-            dma((3 + BLOCKS,)),
-            dma((BLOCKS, 4)),
-            dma((BLOCKS, PLACES)),
+            dma((3 + BLOCKS + TAILS,)),
+            dma((BLOCKS + TAILS, 4)),
+            dma((BLOCKS + TAILS, PLACES)),
             dma((3, 4)),
             dma((3, 4)),
             dma((4,)),
             dma((4,)),
             dma((4,)),
-            dma((2,)),
+            dma((4,)),
             dma((N_CTX,)),
             dma((N_CTX,)),
             dma((N_CTX,)),

time: 179 us -> 186 us (1.039)
  Pallas kernels: 175 us -> 182 us
    pallas_call x1, Pallas kernels: 175 us -> 182 us  [on_device(): pl.pallas_call(kernel, out_shape=(jax.ShapeDtypeStruct((BLK, 8 * HEAD), B...]
where the time goes in v2:
time: 186 us
  Pallas kernels  182 us (98%)
  local copies, waits for them, and re-layouts  2.96 us (2%)
    pallas_call x1, Pallas kernels, on_device(): pl.pallas_call(kernel, out_shape=(jax.ShapeDtypeStruct((BLK, 8 * HEAD), B...  182 us

profile of v2, /device:TPU:2, one launch (start us, length us, event | category | flops | bytes accessed | tf_op | source)
XLA Modules:
  0.0 185.9 jit_solution(16382956341641905926)
XLA Ops:
  0.6 182.3 %star_prefill.1 = (bf16[512,1024]{1,0:T(8,128)(2,1)}, bf16[64,1024]{1,0:T(8,128)(2,1)}) custom-call(bf16[512,1024]{1,0:T(8,128)(2,1)} %x_ref.1, bf16[64,1024]{1,0:T(8,128)(2,1)} %xq_ref.1, bf16[256,1024]{1,0:T(8,128)(2,1)} %wq_ref.1, bf16[256,128]{1,0:T(8,128)(2,1)} %wk_ref.1, bf16[256,128]{1,0:T(8,128)(2,1)} %wv_ref.1, s32[1,64]{1,0:T(1,128)} %bitcast.2, ...), custom_call_target="tpu_custom_call" | custom-call | tf_op jit(solution)/shard_map/star_prefill/pallas_call | solution.py:615
  183.0 0.0 copy-start
  183.0 2.3 %copy.12 = bf16[512,1024]{1,0:T(8,128)(2,1)} copy(bf16[512,1024]{1,0:T(8,128)(2,1)} %get-tuple-element.4) | data formatting | bytes 2097152
  185.3 0.0 copy-done
  185.3 0.7 copy.13
Async XLA Ops:
  183.0 2.3 %copy-start = (bf16[64,1024]{1,0:T(8,128)(2,1)S(1)}, bf16[64,1024]{1,0:T(8,128)(2,1)}, u32[]{:S(2)}) copy-start(bf16[64,1024]{1,0:T(8,128)(2,1)} %get-tuple-element.5) | copy-start | bytes 393220

commit v3 on v1

--- a/solution.py
+++ b/solution.py
@@ -76,9 +76,9 @@
 def kernel(
     x_ref, xq_ref, wq_ref, wk_ref, wv_ref, pos_ref, bound_ref, freq_ref,
     out_ref, qout_ref,
-    w_all, x_all, cos_s, sin_s, acc, kv, akv, q_s, qq_s, part, parts,
+    w_all, x_all, cos_s, sin_s, acc, kv, akv, q_s, qq_s, terms, term_in, part, parts,
     local_sem, w_send, w_recv, x_send, x_recv, sib_send, sib_recv, a_send, a_recv,
-    p_send, p_recv, r_send, r_recv,
+    t_send, t_recv, q_send, q_recv, p_send, p_recv, r_send, r_recv,
 ):
     c = lax.axis_index("ctx")
     t = lax.axis_index("tp")
@@ -280,73 +280,159 @@
         place = column(pos_ref[...].astype(F32))
         angles(BLK, jnp.broadcast_to(place, (QT, HEAD)))
 
-    def rotate(u):
-        return u * cos_s[...] + pltpu.roll(u, HEAD // 2, 1) * sin_s[...]
-
-    def project(b):
-        acc[...] = jnp.zeros_like(acc)
+    def project(weights, first, count, columns):
+        acc[first : first + count, :columns] = jnp.zeros((count, columns), F32)
 
         @pl.loop(0, 8)
         def _(s):
-            acc[...] += jnp.dot(
-                x_all[s],
-                w_all[b, pl.ds(pl.multiple_of(s * FEATS, FEATS), FEATS), :],
+            acc[first : first + count, :columns] += jnp.dot(
+                x_all[s, first : first + count],
+                weights[pl.ds(pl.multiple_of(s * FEATS, FEATS), FEATS), :],
                 preferred_element_type=F32,
             )
 
+    def rotate(first, count, lane):
+        u = acc[first : first + count, lane : lane + HEAD]
+        turned = u * cos_s[first : first + count] + pltpu.roll(u, HEAD // 2, 1) * sin_s[first : first + count]
+        return turned.astype(BF16)
+
     def project_kv():
-        project(0)
-        kv[:, :HEAD] = rotate(acc[:, :HEAD]).astype(BF16)
+        project(w_all.at[0], 0, ROWS, COLS)
+        kv[:, :HEAD] = rotate(0, ROWS, 0)
         kv[:, HEAD:] = acc[:, HEAD:].astype(BF16)
 
-    def project_q(pair):
-        project(pair + 1)
+    def keep_block(head, lane):
+        q_s[head] = rotate(0, BLK, lane)
+
+    def project_pair(pair):
+        project(w_all.at[pair + 1], 0, BLK, COLS)
         for hh in range(2):
-            turned = rotate(acc[:, hh * HEAD : (hh + 1) * HEAD]).astype(BF16)
-            q_s[:, hh * HEAD : (hh + 1) * HEAD] = turned[:BLK]
-            qq_s[pl.ds(pl.multiple_of((pair * 2 + hh) * QT, QT), QT), :] = turned[BLK:]
-
-    def send_part(owner):
+            keep_block(pair * 2 + hh, hh * HEAD)
+
+    def others(act):
+        @pl.loop(1, N_CTX)
+        def _(d):
+            act(lax.rem(c + d, N_CTX))
+
+    def own_rows(n):
+        return pl.ds(pl.multiple_of(n * OWN, OWN), OWN)
+
+    def exchange(source, target, sems, slot, peer):
         return pltpu.make_async_remote_copy(
-            src_ref=part.at[pl.ds(pl.multiple_of(owner * OWN, OWN), OWN)],
-            dst_ref=parts.at[c], send_sem=p_send.at[owner], recv_sem=p_recv.at[c],
-            device_id=(owner, t), device_id_type=MESH,
+            src_ref=source, dst_ref=target, send_sem=sems[0].at[peer], recv_sem=sems[1].at[slot],
+            device_id=(peer, t), device_id_type=MESH,
         )
 
-    def query_part(pair):
-        rows = pl.ds(pl.multiple_of(pair * 2 * QT, 2 * QT), 2 * QT)
-        scores = dot_nt(qq_s[rows, :], kv[:BLK, :HEAD])
+    def term_to(n):
+        return exchange(terms.at[own_rows(n)], term_in.at[c], (t_send, t_recv), c, n)
+
+    def term_from(n):
+        return exchange(terms.at[own_rows(n)], term_in.at[n], (t_send, t_recv), n, n)
+
+    def qq_to(n):
+        return exchange(qq_s.at[own_rows(c)], qq_s.at[own_rows(c)], (q_send, q_recv), c, n)
+
+    def qq_from(n):
+        return exchange(qq_s.at[own_rows(n)], qq_s.at[own_rows(n)], (q_send, q_recv), n, n)
+
+    def part_to(n):
+        return exchange(part.at[n], parts.at[c], (p_send, p_recv), c, n)
+
+    def part_from(n):
+        return exchange(part.at[n], parts.at[n], (p_send, p_recv), n, n)
+
+    def query_terms():
+        share = x_all[lax.div(c, 4), BLK:, pl.ds(pl.multiple_of(lax.rem(c, 4) * SHARD, SHARD), SHARD)]
+        for pair in range(4):
+            term = jnp.dot(share, w_all[pair + 1, own, :], preferred_element_type=F32)
+            terms[pair * 2 * QT : (pair * 2 + 1) * QT, :] = term[:, :HEAD]
+            terms[(pair * 2 + 1) * QT : (pair * 2 + 2) * QT, :] = term[:, HEAD:]
+        term_in[c] = terms[own_rows(c), :]
+        others(lambda n: term_to(n).start())
+
+    def query_sum():
+        others(lambda n: term_from(n).wait_recv())
+        u = jnp.sum(term_in[...], 0)
+        place = pl.ds(pl.multiple_of(BLK + lax.rem(c, QT // OWN) * OWN, OWN), OWN)
+        turned = u * cos_s[place, :] + pltpu.roll(u, HEAD // 2, 1) * sin_s[place, :]
+        qq_s[own_rows(c), :] = turned.astype(BF16)
+        others(lambda n: qq_to(n).start())
+
+    def query_part():
+        others(lambda n: qq_from(n).wait_recv())
         bound = column(bound_ref[...].astype(F32))
-        bound = jnp.concatenate([bound, bound], 0)
-        place = (lax.broadcasted_iota(jnp.int32, scores.shape, 1) + c * BLK).astype(F32)
-        scores = jnp.where(place < bound, scores, NEG)
+        bound = jnp.concatenate([bound] * 2, 0)
+
+        @pl.loop(0, 4)
+        def _(pair):
+            rows = pl.ds(pl.multiple_of(pair * 2 * QT, 2 * QT), 2 * QT)
+            scores = dot_nt(qq_s[rows, :], kv[:BLK, :HEAD])
+            place = (lax.broadcasted_iota(jnp.int32, scores.shape, 1) + c * BLK).astype(F32)
+            scores = jnp.where(place < bound, scores, NEG)
+            peak = jnp.max(scores, 1, keepdims=True)
+            weights = jnp.exp2((scores - peak) * POWER)
+            total = jnp.sum(weights, 1, keepdims=True)
+            mixed = jnp.dot(weights.astype(BF16), kv[:BLK, HEAD:], preferred_element_type=F32)
+            lane = lax.broadcasted_iota(jnp.int32, (8, HEAD), 1)
+            for n in range(8):
+                first = n * OWN
+                part[pair * 8 + n, :OWN, :] = mixed[first : first + OWN]
+                peak_0, peak_1 = peak[first : first + 8], peak[first + 8 : first + 16]
+                total_0, total_1 = total[first : first + 8], total[first + 8 : first + 16]
+                part[pair * 8 + n, OWN:, :] = jnp.where(
+                    lane < 2,
+                    jnp.where(lane == 0, peak_0, peak_1),
+                    jnp.where(lane == 2, total_0, total_1),
+                )
+
+        parts[c] = part[c]
+        others(lambda n: part_to(n).start())
+
+    def result_at(n):
+        return qout_ref.at[
+            pl.ds(pl.multiple_of(lax.rem(n, QT // OWN) * OWN, OWN), OWN),
+            pl.ds(pl.multiple_of(lax.div(n, QT // OWN) * HEAD, HEAD), HEAD),
+        ]
+
+    def result_copy(source, target):
+        piece = result_at(source)
+        return exchange(piece, piece, (r_send, r_recv), source, target)
+
+    def query_merge():
+        others(lambda n: part_from(n).wait_recv())
+
+        def halves(lane):
+            return jnp.concatenate(
+                [parts[:, OWN:, lane : lane + 1], parts[:, OWN:, lane + 1 : lane + 2]], 1
+            )
+
+        peaks = halves(0)
+        top = jnp.max(peaks, 0)
+        scaled = jnp.exp2((peaks - top[None]) * POWER)
+        total_all = jnp.sum(halves(2) * scaled, 0)
+        mixed_all = jnp.sum(parts[:, :OWN, :] * scaled, 0)
+
+        first = lax.rem(c, QT // OWN) * OWN
+        scores = dot_nt(qq_s[own_rows(c), :], kv[BLK:, :HEAD])
+        row = lax.broadcasted_iota(jnp.int32, scores.shape, 0) + first
+        scores = jnp.where(row >= lax.broadcasted_iota(jnp.int32, scores.shape, 1), scores, NEG)
         peak = jnp.max(scores, 1, keepdims=True)
         weights = jnp.exp2((scores - peak) * POWER)
         total = jnp.sum(weights, 1, keepdims=True)
-        mixed = jnp.dot(weights.astype(BF16), kv[:BLK, HEAD:], preferred_element_type=F32)
-        lane = lax.broadcasted_iota(jnp.int32, mixed.shape, 1)
-        part[rows, :HEAD] = mixed
-        part[rows, HEAD:] = jnp.where(lane < HEAD // 2, peak, total)
-
-        @pl.loop(0, 8)
-        def _(n):
-            owner = pair * 8 + n
-
-            @pl.when(owner != c)
-            def _():
-                send_part(owner).start()
-
-            @pl.when(owner == c)
-            def _():
-                parts[c] = part[pl.ds(pl.multiple_of(c * OWN, OWN), OWN), :]
-
-    def attend(pair, hh):
-        head = pair * 2 + hh
+        mixed = jnp.dot(weights.astype(BF16), kv[BLK:, HEAD:], preferred_element_type=F32)
+        final = jnp.maximum(top, peak)
+        w_ctx = jnp.exp2((top - final) * POWER)
+        w_self = jnp.exp2((peak - final) * POWER)
+        done = (mixed_all * w_ctx + mixed * w_self) / (total_all * w_ctx + total * w_self)
+        result_at(c)[...] = done.astype(BF16)
+        others(lambda n: result_copy(c, n).start())
+
+    def attend(head):
         bias = jnp.where(c > 0, 0.0, NEG).astype(F32)
         tile = BLK // 2
         for n in range(2):
             span = (n + 1) * tile
-            q = q_s[n * tile : span, hh * HEAD : (hh + 1) * HEAD]
+            q = q_s[head, n * tile : span, :]
             far = dot_nt(q, akv[:, :HEAD])
             near = dot_nt(q, kv[:span, :HEAD])
             row = lax.broadcasted_iota(jnp.int32, near.shape, 0) + n * tile
@@ -363,6 +449,11 @@
                 mixed / total
             ).astype(BF16)
 
+    def attend_pair(pair):
+        @pl.loop(0, 2)
+        def _(hh):
+            attend(pair * 2 + hh)
+
     depth = jnp.where(y == 3, 1, y) + jnp.minimum(z, NZ - z)
 
     def anchor_copy(first, count, target, line, place):
@@ -372,50 +463,76 @@
             device_id=(target, t), device_id_type=MESH,
         )
 
+    PIECE = BLK // 4
     HALF = BLK // 2
 
-    def anchor_sends(act):
+    def anchor_lines(act):
         @pl.when((z == 0) & (y < 2))
         def _():
-            act(anchor_copy(0, BLK, ctx_at(1, 0), 0, 0))
+            act(ctx_at(1, 0), 0)
 
         @pl.when(c == 0)
         def _():
-            act(anchor_copy(0, BLK, ctx_at(-1, 0), 1, 0))
+            act(ctx_at(-1, 0), 1)
 
         @pl.when(z < 3)
         def _():
-            act(anchor_copy(0, BLK, ctx_at(0, 1), 2, 0))
+            act(ctx_at(0, 1), 2)
+
+        @pl.when((z > 5) | (z == 0))
+        def _():
+            act(ctx_at(0, -1), 3)
+
+    def anchor_piece(k, target, line):
+        return anchor_copy(pl.multiple_of(k * PIECE, PIECE), PIECE, target, line, k)
+
+    def anchor_step(g):
+        k = g - depth
+
+        @pl.when((k >= 0) & (k < 4))
+        def _():
+            @pl.when(depth > 0)
+            def _():
+                anchor_piece(k, ctx_at(0, 1), 2).wait_recv()
+
+            anchor_lines(lambda target, line: anchor_piece(k, target, line).start())
+
+            @pl.when((z == 3) & (k < 2))
+            def _():
+                anchor_piece(k, ctx_at(0, 1), 2).start()
+
+            @pl.when((z == 5) & (k >= 2))
+            def _():
+                anchor_piece(k, ctx_at(0, -1), 3).start()
+
+    def anchor_root():
+        @pl.when(c == 0)
+        def _():
+            akv[...] = kv[:BLK, :]
+
+    def anchor_end():
+        anchor_lines(lambda target, line: anchor_copy(0, BLK, target, line, 0).wait_send())
 
         @pl.when(z == 3)
         def _():
-            act(anchor_copy(0, HALF, ctx_at(0, 1), 2, 0))
-
-        @pl.when((z > 5) | (z == 0))
-        def _():
-            act(anchor_copy(0, BLK, ctx_at(0, -1), 3, 0))
+            anchor_copy(0, HALF, ctx_at(0, 1), 2, 0).wait_send()
 
         @pl.when(z == 5)
         def _():
-            act(anchor_copy(HALF, HALF, ctx_at(0, -1), 3, 1))
-
-    def anchor_pass():
-        @pl.when(z != 4)
-        def _():
-            anchor_copy(0, BLK, ctx_at(0, 1), 2, 0).wait_recv()
-
-        @pl.when(z == 4)
-        def _():
-            anchor_copy(0, HALF, ctx_at(0, 1), 2, 0).wait_recv()
-            anchor_copy(HALF, HALF, ctx_at(0, 1), 2, 1).wait_recv()
-
-        anchor_sends(lambda copy: copy.start())
+            anchor_copy(0, HALF, ctx_at(0, -1), 3, 0).wait_send()
 
     x_first()
 
     @pl.loop(0, BLOCKS + 1)
     def _(j):
         for r in range(4):
+
+            def at(n, *acts):
+                @pl.when(j == n)
+                def _():
+                    for act in acts:
+                        act()
+
             if r < 3:
 
                 @pl.when(j >= 1)
@@ -426,119 +543,41 @@
             def _():
                 step(j, r)
 
-            @pl.when((depth > 0) & (depth == 4 * j + r - 8))
-            def _():
-                anchor_pass()
-
-            @pl.when(j == 0)
-            def _():
-                block_angles(r * (BLK // 4), BLK // 4)
-                if r == 3:
-                    query_angles()
-                    x_second()
-
-            @pl.when(j == 1)
-            def _():
-                if r == 1:
-                    x_third()
-                if r == 3:
-                    x_fourth()
-
             if r == 0:
-
-                @pl.when(j == 2)
-                def _():
-                    x_last()
-                    project_kv()
-
-                    @pl.when(c == 0)
-                    def _():
-                        akv[...] = kv[:BLK, :]
-                        anchor_sends(lambda copy: copy.start())
-
+                at(2, x_last, project_kv, anchor_root)
+
+            anchor_step(4 * j + r - 8)
+
+            at(0, lambda: block_angles(r * (BLK // 4), BLK // 4))
+            if r == 0:
+                at(5, lambda: attend_pair(1))
+            if r == 1:
+                at(1, x_third)
+                at(2, query_terms)
+                at(4, query_merge)
+                at(5, lambda: attend_pair(2))
             if r == 2:
-
-                @pl.when(j == 3)
-                def _():
-                    attend(0, 0)
-                    attend(0, 1)
-
-            if r == 0:
-
-                @pl.when(j >= 4)
-                def _():
-                    attend(j - 3, 0)
-                    attend(j - 3, 1)
-
+                at(3, query_part)
+                at(4, lambda: attend_pair(0))
             if r == 3:
+                at(0, query_angles, x_second)
+                at(1, x_fourth)
+                at(2, query_sum)
 
                 @pl.when(j >= 2)
                 def _():
-                    project_q(j - 2)
-                    query_part(j - 2)
-
-    attend(3, 0)
-    attend(3, 1)
-
-    @pl.loop(0, N_CTX)
-    def _(n):
-        @pl.when(n != c)
-        def _():
-            piece = parts.at[n]
-            pltpu.make_async_remote_copy(
-                src_ref=piece, dst_ref=piece, send_sem=p_send.at[n], recv_sem=p_recv.at[n],
-                device_id=(n, t), device_id_type=MESH,
-            ).wait_recv()
-
-    peaks = parts[:, :, HEAD : HEAD + 1]
-    top = jnp.max(peaks, 0)
-    scaled = jnp.exp2((peaks - top[None]) * POWER)
-    total_all = jnp.sum(parts[:, :, HEAD + HEAD // 2 : HEAD + HEAD // 2 + 1] * scaled, 0)
-    mixed_all = jnp.sum(parts[:, :, :HEAD] * scaled, 0)
-
-    first = lax.rem(c, QT // OWN) * OWN
-    mine = qq_s[pl.ds(pl.multiple_of(c * OWN, OWN), OWN), :]
-    scores = dot_nt(mine, kv[BLK:, :HEAD])
-    row = lax.broadcasted_iota(jnp.int32, scores.shape, 0) + first
-    scores = jnp.where(row >= lax.broadcasted_iota(jnp.int32, scores.shape, 1), scores, NEG)
-    peak = jnp.max(scores, 1, keepdims=True)
-    weights = jnp.exp2((scores - peak) * POWER)
-    total = jnp.sum(weights, 1, keepdims=True)
-    mixed = jnp.dot(weights.astype(BF16), kv[BLK:, HEAD:], preferred_element_type=F32)
-    final = jnp.maximum(top, peak)
-    w_ctx = jnp.exp2((top - final) * POWER)
-    w_self = jnp.exp2((peak - final) * POWER)
-    done = (mixed_all * w_ctx + mixed * w_self) / (total_all * w_ctx + total * w_self)
-
-    def result_at(n):
-        return qout_ref.at[
-            pl.ds(pl.multiple_of(lax.rem(n, QT // OWN) * OWN, OWN), OWN),
-            pl.ds(pl.multiple_of(lax.div(n, QT // OWN) * HEAD, HEAD), HEAD),
-        ]
-
-    def result_copy(source, target):
-        piece = result_at(source)
-        return pltpu.make_async_remote_copy(
-            src_ref=piece, dst_ref=piece, send_sem=r_send.at[target], recv_sem=r_recv.at[source],
-            device_id=(target, t), device_id_type=MESH,
-        )
-
-    result_at(c)[...] = done.astype(BF16)
-
-    @pl.loop(1, N_CTX)
-    def _(d):
-        result_copy(c, lax.rem(c + d, N_CTX)).start()
-
-    @pl.loop(1, N_CTX)
-    def _(d):
-        other = lax.rem(c + d, N_CTX)
-        result_copy(other, other).wait_recv()
-
-    @pl.loop(1, N_CTX)
-    def _(d):
-        other = lax.rem(c + d, N_CTX)
-        result_copy(c, other).wait_send()
-        send_part(other).wait_send()
+                    project_pair(j - 2)
+
+    attend_pair(3)
+    others(lambda n: result_copy(n, n).wait_recv())
+
+    def left(n):
+        term_to(n).wait_send()
+        qq_to(n).wait_send()
+        part_to(n).wait_send()
+        result_copy(c, n).wait_send()
+
+    others(left)
 
     @pl.loop(0, BLOCKS)
     def _(b):
@@ -553,7 +592,7 @@
             x_far(way, chunk, 0).wait_send()
     for dx in (0, 1, -1, 2):
         x_across(dx).wait_send()
-    anchor_sends(lambda copy: copy.wait_send())
+    anchor_end()
 
 
 def on_device(rows, query_rows, positions, bound, wq, wk, wv):
@@ -577,10 +616,12 @@
             pltpu.VMEM((ROWS, COLS), F32),
             pltpu.VMEM((ROWS, COLS), BF16),
             pltpu.VMEM((BLK, COLS), BF16),
-            pltpu.VMEM((BLK, COLS), BF16),
+            pltpu.VMEM((8, BLK, HEAD), BF16),
             pltpu.VMEM((8 * QT, HEAD), BF16),
-            pltpu.VMEM((8 * QT, 2 * HEAD), F32),
-            pltpu.VMEM((N_CTX, OWN, 2 * HEAD), F32),
+            pltpu.VMEM((8 * QT, HEAD), F32),
+            pltpu.VMEM((N_CTX, OWN, HEAD), F32),
+            pltpu.VMEM((N_CTX, OWN + 8, HEAD), F32),
+            pltpu.VMEM((N_CTX, OWN + 8, HEAD), F32),
             dma((3 + BLOCKS,)),
             dma((BLOCKS, 4)),
             dma((BLOCKS, PLACES)),
@@ -589,7 +630,11 @@
             dma((4,)),
             dma((4,)),
             dma((4,)),
-            dma((2,)),
+            dma((4,)),
+            dma((N_CTX,)),
+            dma((N_CTX,)),
+            dma((N_CTX,)),
+            dma((N_CTX,)),
             dma((N_CTX,)),
             dma((N_CTX,)),
             dma((N_CTX,)),

time: 179 us -> 174 us (0.972)
  Pallas kernels: 175 us -> 171 us
    pallas_call x1, Pallas kernels: 175 us -> 171 us  [on_device(): pl.pallas_call(kernel, out_shape=(jax.ShapeDtypeStruct((BLK, 8 * HEAD), B...]
where the time goes in v3:
time: 174 us
  Pallas kernels  171 us (98%)
  local copies, waits for them, and re-layouts  2.96 us (2%)
    pallas_call x1, Pallas kernels, on_device(): pl.pallas_call(kernel, out_shape=(jax.ShapeDtypeStruct((BLK, 8 * HEAD), B...  171 us

profile of v3, /device:TPU:2, one launch (start us, length us, event | category | flops | bytes accessed | tf_op | source)
XLA Modules:
  0.0 174.1 jit_solution(6808221376890113278)
XLA Ops:
  0.6 170.5 %star_prefill.1 = (bf16[512,1024]{1,0:T(8,128)(2,1)}, bf16[64,1024]{1,0:T(8,128)(2,1)}) custom-call(bf16[512,1024]{1,0:T(8,128)(2,1)} %x_ref.1, bf16[64,1024]{1,0:T(8,128)(2,1)} %xq_ref.1, bf16[256,1024]{1,0:T(8,128)(2,1)} %wq_ref.1, bf16[256,128]{1,0:T(8,128)(2,1)} %wk_ref.1, bf16[256,128]{1,0:T(8,128)(2,1)} %wv_ref.1, s32[1,64]{1,0:T(1,128)} %bitcast.2, ...), custom_call_target="tpu_custom_call" | custom-call | tf_op jit(solution)/shard_map/star_prefill/pallas_call | solution.py:603
  171.2 0.0 copy-start
  171.2 2.3 %copy.12 = bf16[512,1024]{1,0:T(8,128)(2,1)} copy(bf16[512,1024]{1,0:T(8,128)(2,1)} %get-tuple-element.4) | data formatting | bytes 2097152
  173.5 0.0 copy-done
  173.5 0.7 copy.13
Async XLA Ops:
  171.2 2.3 %copy-start = (bf16[64,1024]{1,0:T(8,128)(2,1)S(1)}, bf16[64,1024]{1,0:T(8,128)(2,1)}, u32[]{:S(2)}) copy-start(bf16[64,1024]{1,0:T(8,128)(2,1)} %get-tuple-element.5) | copy-start | bytes 393220

commit v4 on v3

--- a/solution.py
+++ b/solution.py
@@ -22,6 +22,9 @@
 COLS = 256
 CHUNK = ROWS // 4
 FEATS = 1024
+STAGGER = 3
+LAG = 2
+ANCHOR_SLOT = 7
 NEG = -1e30
 POWER = math.log2(math.e) / math.sqrt(HEAD)
 OWN = BLK // N_CTX
@@ -43,23 +46,23 @@
     return values
 
 
-def bz_at(way, dist):
-    return way * 4 + dist - 1
-
-
-def by_at(off, way, stage):
-    return 8 + (off % NZ) * 4 + way * 2 + stage - 1
-
-
-def ay_at(way, stage):
-    return 40 + way * 2 + stage - 1
-
-
-def az_at(off, way, dist):
-    return 44 + (off % NY) * 8 + way * 4 + dist - 1
-
-
-PLACES = 76
+def bz_at(dist):
+    return dist - 1
+
+
+def by_at(off, stage):
+    return 4 + (off % NZ) * 2 + stage - 1
+
+
+def ay_at(stage):
+    return 20 + stage - 1
+
+
+def az_at(off, dist):
+    return 22 + (off % NY) * 4 + dist - 1
+
+
+PLACES = 38
 SIGN = (1, -1)
 
 
@@ -76,9 +79,9 @@
 def kernel(
     x_ref, xq_ref, wq_ref, wk_ref, wv_ref, pos_ref, bound_ref, freq_ref,
     out_ref, qout_ref,
-    w_all, x_all, cos_s, sin_s, acc, kv, akv, q_s, qq_s, terms, term_in, part, parts,
+    w_all, x_all, cos_s, sin_s, acc, kv, akv, q_s, qq_s, terms, term_in, mixed_out, mixed_in, level_out, level_in,
     local_sem, w_send, w_recv, x_send, x_recv, sib_send, sib_recv, a_send, a_recv,
-    t_send, t_recv, q_send, q_recv, p_send, p_recv, r_send, r_recv,
+    ex_send, ex_recv,
 ):
     c = lax.axis_index("ctx")
     t = lax.axis_index("tp")
@@ -127,85 +130,78 @@
             first, count = first + (half if way else 0), half
         return pl.ds(pl.multiple_of(origin * SHARD + first, 16), count)
 
-    def w_copy(b, rows, target, line, place):
-        piece = w_all.at[b, rows]
+    def w_copy(blk, rows, target, line, place):
+        piece = w_all.at[blk, rows]
         return pltpu.make_async_remote_copy(
-            src_ref=piece, dst_ref=piece, send_sem=w_send.at[b, line], recv_sem=w_recv.at[b, place],
+            src_ref=piece, dst_ref=piece, send_sem=w_send.at[blk, line], recv_sem=w_recv.at[blk, place],
             device_id=(target, t), device_id_type=MESH,
         )
 
-    def bz(b, way, dist, hop):
+    def bz(blk, way, dist):
         s = SIGN[way]
-        rows = rows_of(ctx_at(0, -s * (dist - 1 + hop)), CUT, REST, dist, 4, way)
-        return w_copy(b, rows, ctx_at(0, s), 2 + way, bz_at(way, dist))
-
-    def by(b, off, way, stage, hop):
+        rows = rows_of(ctx_at(0, -s * (dist - 1)), CUT, REST, dist, 4, way)
+        w_copy(blk, rows, ctx_at(0, s), 2 + way, bz_at(dist)).start()
+
+    def by(blk, off, way, stage):
         s = SIGN[way]
-        rows = rows_of(ctx_at(-s * (stage - 1 + hop), off), CUT, REST, stage, 2, way)
-        return w_copy(b, rows, ctx_at(s, 0), way, by_at(off, way, stage))
-
-    def ay(b, way, stage, hop):
+        rows = rows_of(ctx_at(-s * (stage - 1), off), CUT, REST, stage, 2, way)
+        w_copy(blk, rows, ctx_at(s, 0), way, by_at(off, stage)).start()
+
+    def ay(blk, way, stage):
         s = SIGN[way]
-        rows = rows_of(ctx_at(-s * (stage - 1 + hop), 0), 0, CUT, stage, 2, way)
-        return w_copy(b, rows, ctx_at(s, 0), way, ay_at(way, stage))
-
-    def az(b, off, way, dist, hop):
+        rows = rows_of(ctx_at(-s * (stage - 1), 0), 0, CUT, stage, 2, way)
+        w_copy(blk, rows, ctx_at(s, 0), way, ay_at(stage)).start()
+
+    def az(blk, off, way, dist):
         s = SIGN[way]
-        rows = rows_of(ctx_at(off, -s * (dist - 1 + hop)), 0, CUT, dist, 4, way)
-        return w_copy(b, rows, ctx_at(0, s), 2 + way, az_at(off, way, dist))
-
-    def go(make, *args):
-        make(*args, 0).start()
-
-    def got(make, *args):
-        make(*args, 1).wait_recv()
-
-    def step(b, s):
+        rows = rows_of(ctx_at(off, -s * (dist - 1)), 0, CUT, dist, 4, way)
+        w_copy(blk, rows, ctx_at(0, s), 2 + way, az_at(off, dist)).start()
+
+    def both(make, blk, *args):
+        *front, last = args
+        for way in (0, 1):
+            make(blk, *front, way, last)
+
+    def got(blk, place, count):
+        w_copy(blk, pl.ds(0, count), ctx_at(1, 0), 0, place).wait_recv()
+
+    def step(blk, s):
         if s == 0:
-            for way in (0, 1):
-                go(bz, b, way, 1)
-                go(ay, b, way, 1)
-            for way in (0, 1):
-                go(az, b, 0, way, 1)
-                go(by, b, 0, way, 1)
+            both(bz, blk, 1)
+            both(ay, blk, 1)
+            both(az, blk, 0, 1)
+            both(by, blk, 0, 1)
             return
         if s <= 4:
-            for way in (0, 1):
-                got(bz, b, way, s)
-                if s < 4:
-                    go(bz, b, way, s + 1)
-                    go(by, b, -SIGN[way] * s, 0, 1)
-                    go(by, b, -SIGN[way] * s, 1, 1)
-            if s == 4:
-                go(by, b, 4, 0, 1)
-                go(by, b, 4, 1, 1)
+            got(blk, bz_at(s), 2 * REST if s < 4 else REST)
+            if s < 4:
+                both(bz, blk, s + 1)
+                both(by, blk, -s, 1)
+                both(by, blk, s, 1)
+            else:
+                both(by, blk, 4, 1)
         if s == 1:
-            for way in (0, 1):
-                got(ay, b, way, 1)
-                go(ay, b, way, 2)
-                go(az, b, -SIGN[way], 0, 1)
-                go(az, b, -SIGN[way], 1, 1)
+            got(blk, ay_at(1), 2 * CUT)
+            both(ay, blk, 2)
+            both(az, blk, -1, 1)
+            both(az, blk, 1, 1)
         if s == 2:
-            got(ay, b, 0, 2)
-            got(ay, b, 1, 2)
-            go(az, b, 2, 0, 1)
-            go(az, b, 2, 1, 1)
+            got(blk, ay_at(2), CUT)
+            both(az, blk, 2, 1)
         for off, since in ((0, 0), (1, 1), (-1, 1), (2, 2)):
             dist = s - since
             if 1 <= dist <= 4:
-                for way in (0, 1):
-                    got(az, b, off, way, dist)
-                    if dist < 4:
-                        go(az, b, off, way, dist + 1)
+                got(blk, az_at(off, dist), 2 * CUT if dist < 4 else CUT)
+                if dist < 4:
+                    both(az, blk, off, dist + 1)
         for group in range(5):
             offs = (0,) if group == 0 else (4,) if group == 4 else (-group, group)
             stage = s - group
             if 1 <= stage <= 2:
                 for off in offs:
-                    for way in (0, 1):
-                        got(by, b, off, way, stage)
-                        if stage == 1:
-                            go(by, b, off, way, 2)
+                    got(blk, by_at(off, stage), 2 * REST if stage == 1 else REST)
+                    if stage == 1:
+                        both(by, blk, off, 2)
 
     def x_copy(dx, rows, target, send, recv):
         piece = x_all.at[tp_at(dx), rows]
@@ -280,16 +276,37 @@
         place = column(pos_ref[...].astype(F32))
         angles(BLK, jnp.broadcast_to(place, (QT, HEAD)))
 
-    def project(weights, first, count, columns):
-        acc[first : first + count, :columns] = jnp.zeros((count, columns), F32)
+    def add_slice(b, n, rows):
+        acc[:rows] += jnp.dot(
+            x_all[n, :rows],
+            w_all[b, pl.ds(pl.multiple_of(n * FEATS, FEATS), FEATS), :],
+            preferred_element_type=F32,
+        )
+
+    def project(b, rows):
+        acc[...] = jnp.zeros_like(acc)
 
         @pl.loop(0, 8)
-        def _(s):
-            acc[first : first + count, :columns] += jnp.dot(
-                x_all[s, first : first + count],
-                weights[pl.ds(pl.multiple_of(s * FEATS, FEATS), FEATS), :],
-                preferred_element_type=F32,
-            )
+        def _(n):
+            add_slice(b, n, rows)
+
+    mine, facing = lax.div(z, 4), 1 - lax.div(z, 4)
+
+    def last_slices(*places):
+        for dy, half in places:
+            add_slice(BLOCKS - 1, lax.rem(y + dy + NY, NY) * 2 + half, BLK)
+
+    def last_first():
+        acc[...] = jnp.zeros_like(acc)
+        last_slices((0, mine), (0, facing), (1, mine), (-1, mine))
+
+    def last_second():
+        last_slices((1, facing), (-1, facing), (2, mine))
+
+    def last_third():
+        last_slices((2, facing))
+        for hh in range(2):
+            keep_block(6 + hh, hh * HEAD)
 
     def rotate(first, count, lane):
         u = acc[first : first + count, lane : lane + HEAD]
@@ -297,7 +314,7 @@
         return turned.astype(BF16)
 
     def project_kv():
-        project(w_all.at[0], 0, ROWS, COLS)
+        project(0, ROWS)
         kv[:, :HEAD] = rotate(0, ROWS, 0)
         kv[:, HEAD:] = acc[:, HEAD:].astype(BF16)
 
@@ -305,7 +322,7 @@
         q_s[head] = rotate(0, BLK, lane)
 
     def project_pair(pair):
-        project(w_all.at[pair + 1], 0, BLK, COLS)
+        project(pair + 1, BLK)
         for hh in range(2):
             keep_block(pair * 2 + hh, hh * HEAD)
 
@@ -317,29 +334,32 @@
     def own_rows(n):
         return pl.ds(pl.multiple_of(n * OWN, OWN), OWN)
 
-    def exchange(source, target, sems, slot, peer):
+    def exchange(source, target, kind, peer):
         return pltpu.make_async_remote_copy(
-            src_ref=source, dst_ref=target, send_sem=sems[0].at[peer], recv_sem=sems[1].at[slot],
+            src_ref=source, dst_ref=target, send_sem=ex_send.at[kind], recv_sem=ex_recv.at[kind],
             device_id=(peer, t), device_id_type=MESH,
         )
 
     def term_to(n):
-        return exchange(terms.at[own_rows(n)], term_in.at[c], (t_send, t_recv), c, n)
-
-    def term_from(n):
-        return exchange(terms.at[own_rows(n)], term_in.at[n], (t_send, t_recv), n, n)
+        return exchange(terms.at[own_rows(n)], term_in.at[c], 0, n)
 
     def qq_to(n):
-        return exchange(qq_s.at[own_rows(c)], qq_s.at[own_rows(c)], (q_send, q_recv), c, n)
-
-    def qq_from(n):
-        return exchange(qq_s.at[own_rows(n)], qq_s.at[own_rows(n)], (q_send, q_recv), n, n)
-
-    def part_to(n):
-        return exchange(part.at[n], parts.at[c], (p_send, p_recv), c, n)
-
-    def part_from(n):
-        return exchange(part.at[n], parts.at[n], (p_send, p_recv), n, n)
+        return exchange(qq_s.at[own_rows(c)], qq_s.at[own_rows(c)], 1, n)
+
+    def mixed_to(n):
+        return exchange(mixed_out.at[n], mixed_in.at[c], 2, n)
+
+    def level_to(n):
+        return exchange(level_out.at[n], level_in.at[c], 3, n)
+
+    def result_to(n):
+        return exchange(result_at(c), result_at(c), 4, n)
+
+    def of_all(kind):
+        most = pl.ds(0, N_CTX - 1)
+        rows = pl.ds(0, (N_CTX - 1) * OWN)
+        piece = (term_in.at[most], qq_s.at[rows], mixed_in.at[most], level_in.at[most], qq_s.at[rows])[kind]
+        return exchange(piece, piece, kind, ctx_at(1, 0))
 
     def query_terms():
         share = x_all[lax.div(c, 4), BLK:, pl.ds(pl.multiple_of(lax.rem(c, 4) * SHARD, SHARD), SHARD)]
@@ -351,7 +371,7 @@
         others(lambda n: term_to(n).start())
 
     def query_sum():
-        others(lambda n: term_from(n).wait_recv())
+        of_all(0).wait_recv()
         u = jnp.sum(term_in[...], 0)
         place = pl.ds(pl.multiple_of(BLK + lax.rem(c, QT // OWN) * OWN, OWN), OWN)
         turned = u * cos_s[place, :] + pltpu.roll(u, HEAD // 2, 1) * sin_s[place, :]
@@ -359,7 +379,7 @@
         others(lambda n: qq_to(n).start())
 
     def query_part():
-        others(lambda n: qq_from(n).wait_recv())
+        of_all(1).wait_recv()
         bound = column(bound_ref[...].astype(F32))
         bound = jnp.concatenate([bound] * 2, 0)
 
@@ -376,17 +396,23 @@
             lane = lax.broadcasted_iota(jnp.int32, (8, HEAD), 1)
             for n in range(8):
                 first = n * OWN
-                part[pair * 8 + n, :OWN, :] = mixed[first : first + OWN]
+                mixed_out[pair * 8 + n] = mixed[first : first + OWN].astype(BF16)
                 peak_0, peak_1 = peak[first : first + 8], peak[first + 8 : first + 16]
                 total_0, total_1 = total[first : first + 8], total[first + 8 : first + 16]
-                part[pair * 8 + n, OWN:, :] = jnp.where(
+                level_out[pair * 8 + n] = jnp.where(
                     lane < 2,
                     jnp.where(lane == 0, peak_0, peak_1),
                     jnp.where(lane == 2, total_0, total_1),
                 )
 
-        parts[c] = part[c]
-        others(lambda n: part_to(n).start())
+        mixed_in[c] = mixed_out[c]
+        level_in[c] = level_out[c]
+
+        def both_to(n):
+            mixed_to(n).start()
+            level_to(n).start()
+
+        others(both_to)
 
     def result_at(n):
         return qout_ref.at[
@@ -394,23 +420,20 @@
             pl.ds(pl.multiple_of(lax.div(n, QT // OWN) * HEAD, HEAD), HEAD),
         ]
 
-    def result_copy(source, target):
-        piece = result_at(source)
-        return exchange(piece, piece, (r_send, r_recv), source, target)
-
     def query_merge():
-        others(lambda n: part_from(n).wait_recv())
+        of_all(2).wait_recv()
+        of_all(3).wait_recv()
 
         def halves(lane):
             return jnp.concatenate(
-                [parts[:, OWN:, lane : lane + 1], parts[:, OWN:, lane + 1 : lane + 2]], 1
+                [level_in[:, :, lane : lane + 1], level_in[:, :, lane + 1 : lane + 2]], 1
             )
 
         peaks = halves(0)
         top = jnp.max(peaks, 0)
         scaled = jnp.exp2((peaks - top[None]) * POWER)
         total_all = jnp.sum(halves(2) * scaled, 0)
-        mixed_all = jnp.sum(parts[:, :OWN, :] * scaled, 0)
+        mixed_all = jnp.sum(mixed_in[...].astype(F32) * scaled, 0)
 
         first = lax.rem(c, QT // OWN) * OWN
         scores = dot_nt(qq_s[own_rows(c), :], kv[BLK:, :HEAD])
@@ -425,7 +448,7 @@
         w_self = jnp.exp2((peak - final) * POWER)
         done = (mixed_all * w_ctx + mixed * w_self) / (total_all * w_ctx + total * w_self)
         result_at(c)[...] = done.astype(BF16)
-        others(lambda n: result_copy(c, n).start())
+        others(lambda n: result_to(n).start())
 
     def attend(head):
         bias = jnp.where(c > 0, 0.0, NEG).astype(F32)
@@ -505,6 +528,17 @@
             def _():
                 anchor_piece(k, ctx_at(0, -1), 3).start()
 
+    def all_angles():
+        for n in range(4):
+            block_angles(n * (BLK // 4), BLK // 4)
+        query_angles()
+
+    def heads(pair):
+        return lambda: attend_pair(pair)
+
+    def queries(pair):
+        return lambda: project_pair(pair)
+
     def anchor_root():
         @pl.when(c == 0)
         def _():
@@ -521,63 +555,53 @@
         def _():
             anchor_copy(0, HALF, ctx_at(0, -1), 3, 0).wait_send()
 
+    TASKS = {
+        0: (all_angles,),
+        2: (x_second,),
+        4: (x_third,),
+        6: (x_fourth, x_last, project_kv, anchor_root,),
+        7: (query_terms,),
+        9: (queries(0),),
+        10: (query_sum,),
+        12: (heads(0), queries(1), query_part,),
+        13: (heads(1),),
+        15: (queries(2), query_merge,),
+        16: (last_first,),
+        17: (heads(2), last_second,),
+    }
+
     x_first()
 
-    @pl.loop(0, BLOCKS + 1)
-    def _(j):
-        for r in range(4):
-
-            def at(n, *acts):
-                @pl.when(j == n)
-                def _():
-                    for act in acts:
-                        act()
-
-            if r < 3:
-
-                @pl.when(j >= 1)
-                def _():
-                    step(j - 1, r + 4)
-
-            @pl.when(j < BLOCKS)
-            def _():
-                step(j, r)
-
-            if r == 0:
-                at(2, x_last, project_kv, anchor_root)
-
-            anchor_step(4 * j + r - 8)
-
-            at(0, lambda: block_angles(r * (BLK // 4), BLK // 4))
-            if r == 0:
-                at(5, lambda: attend_pair(1))
-            if r == 1:
-                at(1, x_third)
-                at(2, query_terms)
-                at(4, query_merge)
-                at(5, lambda: attend_pair(2))
-            if r == 2:
-                at(3, query_part)
-                at(4, lambda: attend_pair(0))
-            if r == 3:
-                at(0, query_angles, x_second)
-                at(1, x_fourth)
-                at(2, query_sum)
-
-                @pl.when(j >= 2)
-                def _():
-                    project_pair(j - 2)
-
+    @pl.loop(0, BLOCKS + LAG)
+    def _(i):
+        for r in range(STAGGER):
+            calls = 0
+            for s in reversed(range(7)):
+                if s % STAGGER == r:
+                    b = i - s // STAGGER
+
+                    @pl.when((b >= 0) & (b < BLOCKS))
+                    def _():
+                        step(b, s)
+
+                    if calls < 2:
+                        anchor_step(2 * (STAGGER * i + r - ANCHOR_SLOT) + calls)
+                        calls += 1
+
+            for slot, acts in TASKS.items():
+                if slot % STAGGER == r:
+
+                    @pl.when(i == slot // STAGGER)
+                    def _():
+                        for act in acts:
+                            act()
+
+    last_third()
     attend_pair(3)
-    others(lambda n: result_copy(n, n).wait_recv())
-
-    def left(n):
-        term_to(n).wait_send()
-        qq_to(n).wait_send()
-        part_to(n).wait_send()
-        result_copy(c, n).wait_send()
-
-    others(left)
+    of_all(4).wait_recv()
+
+    for kind in range(5):
+        of_all(kind).wait_send()
 
     @pl.loop(0, BLOCKS)
     def _(b):
@@ -603,8 +627,8 @@
     return pl.pallas_call(
         kernel,
         out_shape=(
-            jax.ShapeDtypeStruct((BLK, 8 * HEAD), BF16),
-            jax.ShapeDtypeStruct((QT, 8 * HEAD), BF16),
+            pltpu.VMEM((BLK, 8 * HEAD), BF16),
+            pltpu.VMEM((QT, 8 * HEAD), BF16),
         ),
         in_specs=[anywhere] * 5 + [vmem] * 3,
         out_specs=(vmem, vmem),
@@ -620,8 +644,10 @@
             pltpu.VMEM((8 * QT, HEAD), BF16),
             pltpu.VMEM((8 * QT, HEAD), F32),
             pltpu.VMEM((N_CTX, OWN, HEAD), F32),
-            pltpu.VMEM((N_CTX, OWN + 8, HEAD), F32),
-            pltpu.VMEM((N_CTX, OWN + 8, HEAD), F32),
+            pltpu.VMEM((N_CTX, OWN, HEAD), BF16),
+            pltpu.VMEM((N_CTX, OWN, HEAD), BF16),
+            pltpu.VMEM((N_CTX, 8, HEAD), F32),
+            pltpu.VMEM((N_CTX, 8, HEAD), F32),
             dma((3 + BLOCKS,)),
             dma((BLOCKS, 4)),
             dma((BLOCKS, PLACES)),
@@ -631,14 +657,8 @@
             dma((4,)),
             dma((4,)),
             dma((4,)),
-            dma((N_CTX,)),
-            dma((N_CTX,)),
-            dma((N_CTX,)),
-            dma((N_CTX,)),
-            dma((N_CTX,)),
-            dma((N_CTX,)),
-            dma((N_CTX,)),
-            dma((N_CTX,)),
+            dma((5,)),
+            dma((5,)),
         ],
         compiler_params=pltpu.CompilerParams(
             collective_id=0, has_side_effects=True, vmem_limit_bytes=56 << 20

time: 174 us -> 161 us (0.925)
  Pallas kernels: 171 us -> 157 us
    pallas_call x1, Pallas kernels: 171 us -> 157 us  [on_device(): pl.pallas_call(kernel, out_shape=(pltpu.VMEM((BLK, 8 * HEAD), BF16), pltp...]
where the time goes in v4:
time: 161 us; the launch traced here: 159 us
  Pallas kernels  157 us (98%)
  local copies, waits for them, and re-layouts  1.63 us (1%)
    pallas_call x1, Pallas kernels, on_device(): pl.pallas_call(kernel, out_shape=(pltpu.VMEM((BLK, 8 * HEAD), BF16), pltp...  157 us

profile of v4, /device:TPU:2, one launch (start us, length us, event | category | flops | bytes accessed | tf_op | source)
XLA Modules:
  0.0 159.5 jit_solution(1142104780881723317)
XLA Ops:
  0.6 157.2 %star_prefill.1 = (bf16[512,1024]{1,0:T(8,128)(2,1)S(1)}, bf16[64,1024]{1,0:T(8,128)(2,1)S(1)}) custom-call(bf16[512,1024]{1,0:T(8,128)(2,1)} %x_ref.1, bf16[64,1024]{1,0:T(8,128)(2,1)} %xq_ref.1, bf16[256,1024]{1,0:T(8,128)(2,1)} %wq_ref.1, bf16[256,128]{1,0:T(8,128)(2,1)} %wk_ref.1, bf16[256,128]{1,0:T(8,128)(2,1)} %wv_ref.1, s32[1,64]{1,0:T(1,128)} %bitcast.2, ...), custom_call_target="tpu_custom_call" | custom-call | tf_op jit(solution)/shard_map/star_prefill/pallas_call | solution.py:627
  157.9 1.0 copy.12
  158.8 0.7 copy.13

commit v5 on v4

--- a/solution.py
+++ b/solution.py
@@ -322,9 +322,12 @@
         q_s[head] = rotate(0, BLK, lane)
 
     def project_pair(pair):
-        project(pair + 1, BLK)
+        project(pair + 1, ROWS if pair < 2 else BLK)
         for hh in range(2):
-            keep_block(pair * 2 + hh, hh * HEAD)
+            head = pair * 2 + hh
+            keep_block(head, hh * HEAD)
+            if pair < 2:
+                qq_s[head * QT : (head + 1) * QT, :] = rotate(BLK, QT, hh * HEAD)
 
     def others(act):
         @pl.loop(1, N_CTX)
@@ -340,11 +343,14 @@
             device_id=(peer, t), device_id_type=MESH,
         )
 
+    def early_rows():
+        return own_rows(N_CTX // 2 + lax.div(c, 2))
+
     def term_to(n):
-        return exchange(terms.at[own_rows(n)], term_in.at[c], 0, n)
+        return exchange(terms.at[own_rows(lax.div(n, 2))], term_in.at[c], 0, n)
 
     def qq_to(n):
-        return exchange(qq_s.at[own_rows(c)], qq_s.at[own_rows(c)], 1, n)
+        return exchange(qq_s.at[early_rows()], qq_s.at[early_rows()], 1, n)
 
     def mixed_to(n):
         return exchange(mixed_out.at[n], mixed_in.at[c], 2, n)
@@ -363,23 +369,47 @@
 
     def query_terms():
         share = x_all[lax.div(c, 4), BLK:, pl.ds(pl.multiple_of(lax.rem(c, 4) * SHARD, SHARD), SHARD)]
-        for pair in range(4):
+        for pair in (2, 3):
             term = jnp.dot(share, w_all[pair + 1, own, :], preferred_element_type=F32)
-            terms[pair * 2 * QT : (pair * 2 + 1) * QT, :] = term[:, :HEAD]
-            terms[(pair * 2 + 1) * QT : (pair * 2 + 2) * QT, :] = term[:, HEAD:]
-        term_in[c] = terms[own_rows(c), :]
-        others(lambda n: term_to(n).start())
+            first = (pair - 2) * 2 * QT
+            terms[first : first + QT, :] = term[:, :HEAD]
+            terms[first + QT : first + 2 * QT, :] = term[:, HEAD:]
+
+        @pl.when(lax.rem(c, 2) == 0)
+        def _():
+            term_in[c] = terms[own_rows(lax.div(c, 2)), :]
+
+        @pl.loop(0, N_CTX // 2)
+        def _(d):
+            n = 2 * lax.rem(lax.div(c, 2) + d, N_CTX // 2)
+
+            @pl.when(n != c)
+            def _():
+                term_to(n).start()
 
     def query_sum():
-        of_all(0).wait_recv()
-        u = jnp.sum(term_in[...], 0)
-        place = pl.ds(pl.multiple_of(BLK + lax.rem(c, QT // OWN) * OWN, OWN), OWN)
-        turned = u * cos_s[place, :] + pltpu.roll(u, HEAD // 2, 1) * sin_s[place, :]
-        qq_s[own_rows(c), :] = turned.astype(BF16)
-        others(lambda n: qq_to(n).start())
+        @pl.when(lax.rem(c, 2) == 0)
+        def _():
+            of_all(0).wait_recv()
+            u = jnp.sum(term_in[...], 0)
+            first = BLK + lax.rem(lax.div(c, 2), QT // OWN) * OWN
+            place = pl.ds(pl.multiple_of(first, OWN), OWN)
+            turned = u * cos_s[place, :] + pltpu.roll(u, HEAD // 2, 1) * sin_s[place, :]
+            qq_s[early_rows(), :] = turned.astype(BF16)
+            others(lambda n: qq_to(n).start())
+
+    def by_parity(kind, even, odd, act):
+        buffer = term_in if kind == 0 else qq_s
+        for parity, count in ((0, even), (1, odd)):
+            if count:
+
+                @pl.when(lax.rem(c, 2) == parity)
+                def _():
+                    piece = buffer.at[pl.ds(0, count if kind == 0 else count * OWN)]
+                    act(exchange(piece, piece, kind, ctx_at(1, 0)))
 
     def query_part():
-        of_all(1).wait_recv()
+        by_parity(1, N_CTX // 2 - 1, N_CTX // 2, lambda copy: copy.wait_recv())
         bound = column(bound_ref[...].astype(F32))
         bound = jnp.concatenate([bound] * 2, 0)
 
@@ -393,17 +423,13 @@
             weights = jnp.exp2((scores - peak) * POWER)
             total = jnp.sum(weights, 1, keepdims=True)
             mixed = jnp.dot(weights.astype(BF16), kv[:BLK, HEAD:], preferred_element_type=F32)
-            lane = lax.broadcasted_iota(jnp.int32, (8, HEAD), 1)
             for n in range(8):
-                first = n * OWN
-                mixed_out[pair * 8 + n] = mixed[first : first + OWN].astype(BF16)
-                peak_0, peak_1 = peak[first : first + 8], peak[first + 8 : first + 16]
-                total_0, total_1 = total[first : first + 8], total[first + 8 : first + 16]
-                level_out[pair * 8 + n] = jnp.where(
-                    lane < 2,
-                    jnp.where(lane == 0, peak_0, peak_1),
-                    jnp.where(lane == 2, total_0, total_1),
-                )
+                mixed_out[pair * 8 + n] = mixed[n * OWN : (n + 1) * OWN].astype(BF16)
+            row = lax.broadcasted_iota(jnp.int32, mixed.shape, 0) & (OWN - 1)
+            lane = lax.broadcasted_iota(jnp.int32, mixed.shape, 1)
+            level = jnp.where(lane == row, peak, jnp.where(lane == row + OWN, total, 0.0))
+            level = jnp.sum(level.reshape(8, OWN, HEAD), 1, keepdims=True)
+            level_out[pl.ds(pl.multiple_of(pair * 8, 8), 8)] = level
 
         mixed_in[c] = mixed_out[c]
         level_in[c] = level_out[c]
@@ -424,15 +450,17 @@
         of_all(2).wait_recv()
         of_all(3).wait_recv()
 
-        def halves(lane):
-            return jnp.concatenate(
-                [level_in[:, :, lane : lane + 1], level_in[:, :, lane + 1 : lane + 2]], 1
-            )
-
-        peaks = halves(0)
+        def levels(first):
+            shape = (N_CTX, OWN, HEAD)
+            row = lax.broadcasted_iota(jnp.int32, shape, 1)
+            lane = lax.broadcasted_iota(jnp.int32, shape, 2)
+            kept = jnp.where(lane == row + first, jnp.broadcast_to(level_in[...], shape), 0.0)
+            return jnp.sum(kept, 2, keepdims=True)
+
+        peaks = levels(0)
         top = jnp.max(peaks, 0)
         scaled = jnp.exp2((peaks - top[None]) * POWER)
-        total_all = jnp.sum(halves(2) * scaled, 0)
+        total_all = jnp.sum(levels(OWN) * scaled, 0)
         mixed_all = jnp.sum(mixed_in[...].astype(F32) * scaled, 0)
 
         first = lax.rem(c, QT // OWN) * OWN
@@ -561,11 +589,13 @@
         4: (x_third,),
         6: (x_fourth, x_last, project_kv, anchor_root,),
         7: (query_terms,),
-        9: (queries(0),),
-        10: (query_sum,),
-        12: (heads(0), queries(1), query_part,),
-        13: (heads(1),),
-        15: (queries(2), query_merge,),
+        9: (query_sum,),
+        10: (queries(0),),
+        11: (heads(0),),
+        12: (queries(1),),
+        13: (query_part,),
+        14: (heads(1),),
+        15: (query_merge, queries(2),),
         16: (last_first,),
         17: (heads(2), last_second,),
     }
@@ -600,7 +630,9 @@
     attend_pair(3)
     of_all(4).wait_recv()
 
-    for kind in range(5):
+    by_parity(0, N_CTX // 2 - 1, N_CTX // 2, lambda copy: copy.wait_send())
+    by_parity(1, N_CTX - 1, 0, lambda copy: copy.wait_send())
+    for kind in (2, 3, 4):
         of_all(kind).wait_send()
 
     @pl.loop(0, BLOCKS)
@@ -642,12 +674,12 @@
             pltpu.VMEM((BLK, COLS), BF16),
             pltpu.VMEM((8, BLK, HEAD), BF16),
             pltpu.VMEM((8 * QT, HEAD), BF16),
-            pltpu.VMEM((8 * QT, HEAD), F32),
+            pltpu.VMEM((4 * QT, HEAD), F32),
             pltpu.VMEM((N_CTX, OWN, HEAD), F32),
             pltpu.VMEM((N_CTX, OWN, HEAD), BF16),
             pltpu.VMEM((N_CTX, OWN, HEAD), BF16),
-            pltpu.VMEM((N_CTX, 8, HEAD), F32),
-            pltpu.VMEM((N_CTX, 8, HEAD), F32),
+            pltpu.VMEM((N_CTX, 1, HEAD), F32),
+            pltpu.VMEM((N_CTX, 1, HEAD), F32),
             dma((3 + BLOCKS,)),
             dma((BLOCKS, 4)),
             dma((BLOCKS, PLACES)),

time: 161 us -> 156 us (0.969)
  the two profiles are of different devices: /device:TPU:2 before, /device:TPU:1 now
where the time goes in v5:
time: 156 us
  Pallas kernels  153 us (98%)
  local copies, waits for them, and re-layouts  1.63 us (1%)
    pallas_call x1, Pallas kernels, on_device(): pl.pallas_call(kernel, out_shape=(pltpu.VMEM((BLK, 8 * HEAD), BF16), pltp...  153 us

profile of v5, /device:TPU:1, one launch (start us, length us, event | category | flops | bytes accessed | tf_op | source)
XLA Modules:
  0.0 155.7 jit_solution(12412113183005247525)
XLA Ops:
  0.6 153.4 %star_prefill.1 = (bf16[512,1024]{1,0:T(8,128)(2,1)S(1)}, bf16[64,1024]{1,0:T(8,128)(2,1)S(1)}) custom-call(bf16[512,1024]{1,0:T(8,128)(2,1)} %x_ref.1, bf16[64,1024]{1,0:T(8,128)(2,1)} %xq_ref.1, bf16[256,1024]{1,0:T(8,128)(2,1)} %wq_ref.1, bf16[256,128]{1,0:T(8,128)(2,1)} %wk_ref.1, bf16[256,128]{1,0:T(8,128)(2,1)} %wv_ref.1, s32[1,64]{1,0:T(1,128)} %bitcast.2, ...), custom_call_target="tpu_custom_call" | custom-call | tf_op jit(solution)/shard_map/star_prefill/pallas_call | solution.py:659
  154.0 1.0 copy.12
  155.0 0.7 copy.13

commit v6 on v5

--- a/solution.py
+++ b/solution.py
@@ -514,7 +514,7 @@
             device_id=(target, t), device_id_type=MESH,
         )
 
-    PIECE = BLK // 4
+    PIECE = BLK // 2
     HALF = BLK // 2
 
     def anchor_lines(act):
@@ -540,7 +540,7 @@
     def anchor_step(g):
         k = g - depth
 
-        @pl.when((k >= 0) & (k < 4))
+        @pl.when((k >= 0) & (k < 2))
         def _():
             @pl.when(depth > 0)
             def _():
@@ -548,11 +548,11 @@
 
             anchor_lines(lambda target, line: anchor_piece(k, target, line).start())
 
-            @pl.when((z == 3) & (k < 2))
+            @pl.when((z == 3) & (k < 1))
             def _():
                 anchor_piece(k, ctx_at(0, 1), 2).start()
 
-            @pl.when((z == 5) & (k >= 2))
+            @pl.when((z == 5) & (k >= 1))
             def _():
                 anchor_piece(k, ctx_at(0, -1), 3).start()
 
@@ -591,12 +591,11 @@
         7: (query_terms,),
         9: (query_sum,),
         10: (queries(0),),
-        11: (heads(0),),
         12: (queries(1),),
         13: (query_part,),
-        14: (heads(1),),
+        14: (heads(0),),
         15: (query_merge, queries(2),),
-        16: (last_first,),
+        16: (last_first, heads(1),),
         17: (heads(2), last_second,),
     }
 
@@ -605,7 +604,6 @@
     @pl.loop(0, BLOCKS + LAG)
     def _(i):
         for r in range(STAGGER):
-            calls = 0
             for s in reversed(range(7)):
                 if s % STAGGER == r:
                     b = i - s // STAGGER
@@ -614,9 +612,7 @@
                     def _():
                         step(b, s)
 
-                    if calls < 2:
-                        anchor_step(2 * (STAGGER * i + r - ANCHOR_SLOT) + calls)
-                        calls += 1
+            anchor_step(STAGGER * i + r - ANCHOR_SLOT)
 
             for slot, acts in TASKS.items():
                 if slot % STAGGER == r:

time: 156 us -> 154 us (0.987)
  Pallas kernels: 153 us -> 151 us
    pallas_call x1, Pallas kernels: 153 us -> 151 us  [on_device(): pl.pallas_call(kernel, out_shape=(pltpu.VMEM((BLK, 8 * HEAD), BF16), pltp...]
where the time goes in v6:
time: 154 us
  Pallas kernels  151 us (98%)
  local copies, waits for them, and re-layouts  1.63 us (1%)
    pallas_call x1, Pallas kernels, on_device(): pl.pallas_call(kernel, out_shape=(pltpu.VMEM((BLK, 8 * HEAD), BF16), pltp...  151 us

profile of v6, /device:TPU:1, one launch (start us, length us, event | category | flops | bytes accessed | tf_op | source)
XLA Modules:
  0.0 153.7 jit_solution(9704625633343233251)
XLA Ops:
  0.6 151.4 %star_prefill.1 = (bf16[512,1024]{1,0:T(8,128)(2,1)S(1)}, bf16[64,1024]{1,0:T(8,128)(2,1)S(1)}) custom-call(bf16[512,1024]{1,0:T(8,128)(2,1)} %x_ref.1, bf16[64,1024]{1,0:T(8,128)(2,1)} %xq_ref.1, bf16[256,1024]{1,0:T(8,128)(2,1)} %wq_ref.1, bf16[256,128]{1,0:T(8,128)(2,1)} %wk_ref.1, bf16[256,128]{1,0:T(8,128)(2,1)} %wv_ref.1, s32[1,64]{1,0:T(1,128)} %bitcast.2, ...), custom_call_target="tpu_custom_call" | custom-call | tf_op jit(solution)/shard_map/star_prefill/pallas_call | solution.py:655
  152.0 1.0 copy.12
  153.0 0.7 copy.13

commit v7 on v6

--- a/solution.py
+++ b/solution.py
@@ -114,13 +114,11 @@
 
     barrier = pltpu.get_barrier_semaphore()
 
-    @pl.loop(1, N_CTX)
-    def _(d):
-        pl.semaphore_signal(barrier, inc=1, device_id=(lax.rem(c + d, N_CTX), t), device_id_type=MESH)
-
+    for near in (ctx_at(1, 0), ctx_at(-1, 0), ctx_at(0, 1), ctx_at(0, -1)):
+        pl.semaphore_signal(barrier, inc=1, device_id=(near, t), device_id_type=MESH)
     for other in (tp_at(1), tp_at(-1), sibling):
         pl.semaphore_signal(barrier, inc=1, device_id=(c, other), device_id_type=MESH)
-    pl.semaphore_wait(barrier, N_CTX - 1 + 3)
+    pl.semaphore_wait(barrier, 7)
     for copy in locals_:
         copy.wait()
 
@@ -623,7 +621,8 @@
                             act()
 
     last_third()
-    attend_pair(3)
+    attend(6)
+    attend(7)
     of_all(4).wait_recv()
 
     by_parity(0, N_CTX // 2 - 1, N_CTX // 2, lambda copy: copy.wait_send())

time: 154 us -> 152 us (0.987)
    pallas_call x1, Pallas kernels: 151 us -> 150 us  [on_device(): pl.pallas_call(kernel, out_shape=(pltpu.VMEM((BLK, 8 * HEAD), BF16), pltp...]
where the time goes in v7:
time: 152 us
  Pallas kernels  150 us (99%)
  local copies, waits for them, and re-layouts  1.63 us (1%)
    pallas_call x1, Pallas kernels, on_device(): pl.pallas_call(kernel, out_shape=(pltpu.VMEM((BLK, 8 * HEAD), BF16), pltp...  150 us

profile of v7, /device:TPU:1, one launch (start us, length us, event | category | flops | bytes accessed | tf_op | source)
XLA Modules:
  0.0 152.0 jit_solution(13673387882189308434)
XLA Ops:
  0.6 149.7 %star_prefill.1 = (bf16[512,1024]{1,0:T(8,128)(2,1)S(1)}, bf16[64,1024]{1,0:T(8,128)(2,1)S(1)}) custom-call(bf16[512,1024]{1,0:T(8,128)(2,1)} %x_ref.1, bf16[64,1024]{1,0:T(8,128)(2,1)} %xq_ref.1, bf16[256,1024]{1,0:T(8,128)(2,1)} %wq_ref.1, bf16[256,128]{1,0:T(8,128)(2,1)} %wk_ref.1, bf16[256,128]{1,0:T(8,128)(2,1)} %wv_ref.1, s32[1,64]{1,0:T(1,128)} %bitcast.2, ...), custom_call_target="tpu_custom_call" | custom-call | tf_op jit(solution)/shard_map/star_prefill/pallas_call | solution.py:654
  150.3 1.0 copy.12
  151.3 0.7 copy.13
